TPU v7x, 32 devices: a whole 2x2x4 slice. The times are simulated.
32 devices in a mesh: gx: 8 (over z, y), gy: 4 (over x, core).
Axes of the slice: x: 2, y: 2, z: 4, core: 2. Of those that a mesh axis runs over, the one named last changes fastest.
Arguments:
- disp: bfloat16 [2048, 4096], P(('gx', 'gy')), may hold values from -6 to 6
- adjoint: bfloat16 [2048, 4096], P(('gx', 'gy')), may hold values from -6 to 6
- tiles: bfloat16 [3072, 4096], P(('gx', 'gy')), may hold values from -0.75 to 0.75
- tile_rows: int32 [3072], P(('gx', 'gy')), may hold values from 0 to 63
- tile_cols: int32 [3072], P(('gx', 'gy')), may hold values from 0 to 95
- density: float32 [3072], P(('gx', 'gy')), may hold values from 0.1 to 1
- filter_weight: float32 [3072], P(('gx', 'gy')), may hold values from 0.2 to 2
- owner: int32 [3072, 1], P(('gx', 'gy')), may hold values from 0 to 3; in each aligned block of 96 rows (0 to 95, 96 to 191, ...) at most 96 rows name the same one
- region: int32 [3072], P(('gx', 'gy')), may hold values from 0 to 31
- face_x: int32 [32, 2, 12], P(('gx', 'gy')), may hold values from 0 to 63
- face_y: int32 [32, 2, 4], P(('gx', 'gy')), may hold values from 0 to 63
Outputs:
- filtered: float32 [1024, 128], P(('gx', 'gy'))
- compliance: float32 [64], replicated
Inputs may be any that keep to these rules, and one draw needn't show every extreme that they name: Among the 96 elements of one subdomain at most 96 name the same owner, a bound that some block reaches.
All inputs are finite; a program needn't handle non-finite values.
Results may differ from a plain program's by a relative error of at most 0.0005.
Values may be sent and summed in bfloat16 or wider, within the bound.
A program may use at most 64 MiB of HBM per device.

v0:
```python
import math

import jax
import jax.numpy as jnp
from jax import lax
from jax.sharding import PartitionSpec as P

BS = 64
R = 64
NREG = 32
CAP = 96


def shifted(x, axis, by):
    size = lax.axis_size(axis)
    pairs = [(i, i + by) for i in range(size) if 0 <= i + by < size]
    return lax.ppermute(x, axis, pairs)


def across_columns(first, second, by):
    return shifted((first, second), "gx", by)


def across_rows(first, second, by):
    return shifted((first, second), "gy", by)


def shards(
    disp,
    adjoint,
    tiles,
    tile_rows,
    tile_cols,
    density,
    filter_weight,
    owner,
    region,
    face_x,
    face_y,
):
    lists_x = face_x[0]
    lists_y = face_y[0]
    low_x = across_columns(disp[lists_x[0]], adjoint[lists_x[0]], 1)
    high_x = across_columns(disp[lists_x[1]], adjoint[lists_x[1]], -1)
    low_y = across_rows(disp[lists_y[0]], adjoint[lists_y[0]], 1)
    high_y = across_rows(disp[lists_y[1]], adjoint[lists_y[1]], -1)
    disp_ext = jnp.concatenate([disp, low_x[0], high_x[0], low_y[0], high_y[0]], axis=0)
    adj_ext = jnp.concatenate([adjoint, low_x[1], high_x[1], low_y[1], high_y[1]], axis=0)
    count = tiles.shape[0]
    kmat = tiles.reshape(count, BS, BS)
    ucol = disp_ext[tile_cols].reshape(count, BS, R)
    lcol = adj_ext[tile_cols].reshape(count, BS, R)
    ku = jnp.einsum("tjk,tkr->tjr", kmat, ucol, preferred_element_type=jnp.float32)
    kl = jnp.einsum("tjk,tkr->tjr", kmat, lcol, preferred_element_type=jnp.float32)
    urow = disp[tile_rows].reshape(count, BS, R).astype(jnp.float32)
    lrow = adjoint[tile_rows].reshape(count, BS, R).astype(jnp.float32)
    cross = jnp.sum(lrow * ku + urow * kl, axis=1)
    energy = jnp.sum(urow * ku, axis=1) / math.sqrt(BS)
    sens = -(3.0 * density * density / (2.0 * math.sqrt(BS)))[:, None] * cross
    payload = filter_weight[:, None] * jnp.concatenate([sens, energy], axis=1)
    rows_y = lax.axis_size("gy")
    total_tiles = count * lax.axis_size("gx") * rows_y
    compliance = lax.psum(jnp.sum(energy, axis=0), ("gx", "gy")) / math.sqrt(total_tiles)
    target = owner[:, 0]
    onehot = (target[:, None] == jnp.arange(rows_y, dtype=jnp.int32)[None, :]).astype(jnp.int32)
    before = jnp.cumsum(onehot, axis=0) - onehot
    slot = jnp.sum(before * onehot, axis=1)
    position = target * CAP + slot
    buffer = jnp.zeros((rows_y * CAP, 2 * R), jnp.float32).at[position].set(payload)
    weights = jnp.zeros((rows_y * CAP,), jnp.float32).at[position].set(filter_weight)
    labels = jnp.full((rows_y * CAP,), NREG, jnp.int32).at[position].set(region)
    got_rows, got_weights = (
        lax.all_to_all(
            buffer.reshape(rows_y, CAP, 2 * R), "gy", split_axis=0, concat_axis=0, tiled=True
        ),
        lax.all_to_all(weights.reshape(rows_y, CAP), "gy", split_axis=0, concat_axis=0, tiled=True),
    )
    got_labels = lax.all_to_all(
        labels.reshape(rows_y, CAP), "gy", split_axis=0, concat_axis=0, tiled=True
    )
    flat_labels = got_labels.reshape(-1)
    sums = jax.ops.segment_sum(got_rows.reshape(-1, 2 * R), flat_labels, NREG + 1)[:NREG]
    totals = jax.ops.segment_sum(got_weights.reshape(-1), flat_labels, NREG + 1)[:NREG]
    filtered = sums / jnp.maximum(totals, 1.0)[:, None]
    return (filtered, compliance)


def solution(mesh):
    placed = (
        P(("gx", "gy"), None),
        P(("gx", "gy"), None),
        P(("gx", "gy"), None),
        P(("gx", "gy")),
        P(("gx", "gy")),
        P(("gx", "gy")),
        P(("gx", "gy")),
        P(("gx", "gy"), None),
        P(("gx", "gy")),
        P(("gx", "gy"), None, None),
        P(("gx", "gy"), None, None),
    )
    return jax.shard_map(
        shards, mesh=mesh, in_specs=placed, out_specs=(P(("gx", "gy"), None), P()), check_vma=False
    )
```

profile of v0, /device:TPU:0, one launch (start us, length us, event | category | flops | bytes accessed | tf_op | source)
XLA Modules:
  0.0 145.6 jit_solution(2420739111669740940)
XLA Ops:
  4.9 4.2 %all-to-all-start = ((s32[4,1,96]{2,1,0:T(1,128)}), s32[4,1,96]{2,1,0:T(1,128)S(1)}, u32[]{:S(2)}, u32[]{:S(2)}) async-start(s32[4,1,96]{2,1,0:T(1,128)} %all_to_all.15), calls=%async_computation | async-start | bytes 4096 | tf_op jit(solution)/shard_map/all_to_all | solution.py:78
  9.8 2.4 %gather_fusion.1 = bf16[12,4096]{1,0:T(8,128)(2,1)} fusion(bf16[64,4096]{1,0:T(8,128)(2,1)} %param.11, s32[1024]{0:T(1024)S(1)} %pad_clamp_fusion.4), kind=kCustom, calls=%fused_computation.1 | custom fusion | bytes 196656 | tf_op jit(solution)/shard_map/gather | solution.py:43
  12.3 3.9 %collective-permute-start = (bf16[12,4096]{1,0:T(8,128)(2,1)}, bf16[12,4096]{1,0:T(8,128)(2,1)S(1)}, u32[]{:S(2)}, u32[]{:S(2)}) collective-permute-start(bf16[12,4096]{1,0:T(8,128)(2,1)} %gather_fusion.1), channel_id=1, source_target_pairs={{0,4},{4,8},{8,12},{12,16},{16,20},{20,24},{24,28},{1,5},{5,9},{9,... | collective-permute-start | bytes 294920 | tf_op jit(solution)/shard_map/ppermute | solution.py:17
  20.0 2.7 %collective-permute-start.2 = (bf16[4,4096]{1,0:T(4,128)(2,1)}, bf16[4,4096]{1,0:T(4,128)(2,1)}, u32[]{:S(2)}, u32[]{:S(2)}) collective-permute-start(bf16[4,4096]{1,0:T(4,128)(2,1)} %gather_fusion.3), channel_id=1, source_target_pairs={{0,1},{1,2},{2,3},{4,5},{5,6},{6,7},{8,9},{9,10},{10,11},{12,13},{... | collective-permute-start | bytes 98312 | tf_op jit(solution)/shard_map/ppermute | solution.py:17
  26.4 4.3 %collective-permute-start.4 = (bf16[12,4096]{1,0:T(8,128)(2,1)}, bf16[12,4096]{1,0:T(8,128)(2,1)S(1)}, u32[]{:S(2)}, u32[]{:S(2)}) collective-permute-start(bf16[12,4096]{1,0:T(8,128)(2,1)} %gather_fusion.7), channel_id=1, source_target_pairs={{0,4},{4,8},{8,12},{12,16},{16,20},{20,24},{24,28},{1,5},{5,9},{9,... | collective-permute-start | bytes 294920 | tf_op jit(solution)/shard_map/ppermute | solution.py:17
  33.0 5.1 %all-to-all-start.2 = ((f32[4,1,96]{2,1,0:T(1,128)}), f32[4,1,96]{2,1,0:T(1,128)S(1)}, u32[]{:S(2)}, u32[]{:S(2)}) async-start(f32[4,1,96]{2,1,0:T(1,128)} %all_to_all.18), calls=%async_computation.2 | async-start | bytes 4096 | tf_op jit(solution)/shard_map/all_to_all | solution.py:76
  38.1 1.9 %gather_fusion.6 = bf16[96,4096]{1,0:T(8,128)(2,1)} fusion(bf16[64,4096]{1,0:T(8,128)(2,1)S(1)} %copy-done, s32[1024]{0:T(1024)S(1)} %pad_clamp_fusion.5), kind=kCustom, calls=%fused_computation.6 | custom fusion | bytes 1573248 | tf_op jit(solution)/shard_map/gather | solution.py:55
  40.0 1.9 %gather_fusion = bf16[96,4096]{1,0:T(8,128)(2,1)} fusion(bf16[64,4096]{1,0:T(8,128)(2,1)S(1)} %copy-done.1, s32[1024]{0:T(1024)S(1)} %pad_clamp_fusion.5), kind=kCustom, calls=%fused_computation | custom fusion | bytes 1573248 | tf_op jit(solution)/shard_map/gather | solution.py:56
  47.0 3.7 %copy.23 = f32[96,64,64]{2,1,0:T(8,128)} copy(f32[96,64,64]{0,2,1:T(8,128)S(1)} %bitcast.47) | data formatting | bytes 3145728 | tf_op jit(solution)/shard_map/convert_element_type | solution.py:55
  50.7 1.6 %copy.15 = bf16[96,4096]{0,1:T(8,128)(2,1)S(1)} copy(bf16[96,4096]{1,0:T(8,128)(2,1)} %param.13) | data formatting | bytes 1572864 | tf_op args[2]
  52.3 3.1 %copy.17 = bf16[96,64,64]{2,1,0:T(8,128)(2,1)} copy(bf16[96,64,64]{0,2,1:T(8,128)(2,1)S(1)} %bitcast.51) | data formatting | bytes 1572864 | tf_op jit(solution)/shard_map/reshape | solution.py:50
  56.8 3.7 %copy.18 = f32[96,64,64]{2,1,0:T(8,128)} copy(f32[96,64,64]{0,2,1:T(8,128)S(1)} %bitcast.48) | data formatting | bytes 3145728 | tf_op jit(solution)/shard_map/convert_element_type | solution.py:56
  63.0 3.9 %scatter_custom_fusion.4 = f32[33]{0:T(128)S(1)} fusion(s32[384]{0:T(512)S(1)} %reshape.285, f32[384]{0:T(512)S(1)} %reshape.303, f32[]{:T(128)} %constant.11.clone.1), kind=kCustom, calls=%fused_computation.65 | custom fusion | flops 384 | bytes 136 | tf_op jit(solution)/shard_map/scatter-add | solution.py:83
  68.2 2.4 %collective-permute-start.6 = (bf16[4,4096]{1,0:T(4,128)(2,1)}, bf16[4,4096]{1,0:T(4,128)(2,1)S(1)}, u32[]{:S(2)}, u32[]{:S(2)}) collective-permute-start(bf16[4,4096]{1,0:T(4,128)(2,1)} %gather_fusion.9), channel_id=1, source_target_pairs={{0,1},{1,2},{2,3},{4,5},{5,6},{6,7},{8,9},{9,10},{10,11},{12,13},{... | collective-permute-start | bytes 98312 | tf_op jit(solution)/shard_map/ppermute | solution.py:17
  70.6 1.5 %collective-permute-start.7 = (bf16[4,4096]{1,0:T(4,128)(2,1)}, bf16[4,4096]{1,0:T(4,128)(2,1)S(1)}, u32[]{:S(2)}, u32[]{:S(2)}) collective-permute-start(bf16[4,4096]{1,0:T(4,128)(2,1)} %gather_fusion.10), channel_id=1, source_target_pairs={{1,0},{2,1},{3,2},{5,4},{6,5},{7,6},{9,8},{10,9},{11,10},{13,12},{... | collective-permute-start | bytes 98312 | tf_op jit(solution)/shard_map/ppermute | solution.py:17
  75.1 3.1 %copy.16 = bf16[96,64,64]{2,1,0:T(8,128)(2,1)} copy(bf16[96,64,64]{0,2,1:T(8,128)(2,1)S(1)} %bitcast.49) | data formatting | bytes 1572864 | tf_op jit(solution)/shard_map/reshape | solution.py:51
  78.8 1.9 %gather_fusion.11 = bf16[96,4096]{1,0:T(8,128)(2,1)} fusion(bf16[96,4096]{1,0:T(8,128)(2,1)S(1)} %concatenate.10, s32[1024]{0:T(1024)S(1)} %pad_clamp_fusion), kind=kCustom, calls=%fused_computation.11 | custom fusion | bytes 1573248 | tf_op jit(solution)/shard_map/gather | solution.py:52
  80.7 2.4 %copy.20 = bf16[96,4096]{0,1:T(8,128)(2,1)} copy(bf16[96,4096]{1,0:T(8,128)(2,1)} %gather_fusion.11) | data formatting | bytes 1572864 | tf_op jit(solution)/shard_map/gather | solution.py:52
  83.1 4.0 %copy.21 = bf16[96,64,64]{2,1,0:T(8,128)(2,1)} copy(bf16[96,64,64]{0,2,1:T(8,128)(2,1)} %bitcast.50) | data formatting | bytes 1572864 | tf_op jit(solution)/shard_map/reshape | solution.py:52
  87.1 2.6 %fusion.2 = (f32[96,64]{1,0:T(8,128)S(1)}, f32[96,64,64]{1,2,0:T(8,128)S(1)}) fusion(f32[96,64,64]{2,1,0:T(8,128)S(1)} %copy-done.2, bf16[96,64,64]{2,1,0:T(8,128)(2,1)} %copy.17, bf16[96,64,64]{2,1,0:T(8,128)(2,1)} %copy.16), kind=kOutput, calls=%fused_computation.22 | convolution fusion | flops 51111936 | bytes 4743168 | tf_op jit(solution)/shard_map/tjk,tkr->tjr/dot_general | solution.py:53
  91.8 1.7 %scatter_custom_fusion.1 = f32[384,128]{1,0:T(8,128)} fusion(s32[96]{0:T(128)} %copy-done.12, f32[]{:T(128)} %constant.11.clone.1, f32[96,64]{1,0:T(8,128)S(1)} %get-tuple-element.3, f32[]{:T(128)} %constant.44, f32[96,64]{1,0:T(8,128)S(1)} %get-tuple-element.10, f32[96]{0:T(128)S(1)} %copy-done.7), kind=kCustom, calls=%fused_computation.23 | custom fusion | flops 24576 | bytes 247168 | tf_op jit(solution)/shard_map/scatter | solution.py:69
  93.5 5.1 %all-to-all-start.1 = ((f32[4,96,128]{2,1,0:T(8,128)}), f32[4,96,128]{2,1,0:T(8,128)S(1)}, u32[]{:S(2)}, u32[]{:S(2)}) async-start(f32[4,96,128]{2,1,0:T(8,128)} %bitcast.18), calls=%async_computation.1 | async-start | bytes 393216 | tf_op jit(solution)/shard_map/all_to_all | solution.py:73
  98.6 42.7 %psum.7 = f32[64]{0:T(128)S(1)} all-reduce(f32[64]{0:T(128)S(1)} %get-tuple-element.2), channel_id=1, replica_groups=mesh['gx'=8,'gy'=4] {'gx','gy'}, use_global_device_ids=true, to_apply=%region_10.11 | all-reduce | flops 64 | bytes 512 | tf_op jit(solution)/shard_map/psum | solution.py:63
  141.9 3.0 %scatter_custom_fusion.2 = f32[33,128]{1,0:T(8,128)S(1)} fusion(s32[384]{0:T(512)S(1)} %reshape.285, f32[384,128]{1,0:T(8,128)S(1)} %bitcast.52, f32[]{:T(128)} %constant.11.clone.1), kind=kCustom, calls=%fused_computation.35 | custom fusion | flops 49152 | bytes 16900 | tf_op jit(solution)/shard_map/scatter-add | solution.py:82
  (83 shorter events, 31.7 us)
Async XLA Ops:
  0.6 15.6 %copy-start = (bf16[64,4096]{1,0:T(8,128)(2,1)S(1)}, bf16[64,4096]{1,0:T(8,128)(2,1)}, u32[]{:S(2)}) copy-start(bf16[64,4096]{1,0:T(8,128)(2,1)} %param.11) | copy-start | bytes 1572868
  0.6 18.1 %copy-start.6 = (s32[1,2,4]{2,1,0:T(2,128)S(1)}, s32[1,2,4]{2,1,0:T(2,128)}, u32[]{:S(2)}) copy-start(s32[1,2,4]{2,1,0:T(2,128)} %param.21) | copy-start | bytes 100
  0.7 24.5 %copy-start.1 = (bf16[64,4096]{1,0:T(8,128)(2,1)S(1)}, bf16[64,4096]{1,0:T(8,128)(2,1)}, u32[]{:S(2)}) copy-start(bf16[64,4096]{1,0:T(8,128)(2,1)} %param.12) | copy-start | bytes 1572868
  2.5 28.2 %copy-start.9 = (s32[96]{0:T(128)S(1)}, s32[96]{0:T(128)}, u32[]{:S(2)}) copy-start(s32[96]{0:T(128)} %param.14) | copy-start | bytes 1156
  2.5 28.2 %copy-start.10 = (s32[96]{0:T(128)S(1)}, s32[96]{0:T(128)}, u32[]{:S(2)}) copy-start(s32[96]{0:T(128)} %param.15) | copy-start | bytes 1156
  2.5 28.2 %copy-start.11 = (f32[96]{0:T(128)S(1)}, f32[96]{0:T(128)}, u32[]{:S(2)}) copy-start(f32[96]{0:T(128)} %param.16) | copy-start | bytes 1156
  3.2 34.9 %copy-start.12 = (s32[96]{0:T(128)}, s32[96]{0:T(128)S(1)}, u32[]{:S(2)}) copy-start(s32[96]{0:T(128)S(1)} %fusion.17) | copy-start | bytes 1156
  4.9 28.1 %all-to-all-start = ((s32[4,1,96]{2,1,0:T(1,128)}), s32[4,1,96]{2,1,0:T(1,128)S(1)}, u32[]{:S(2)}, u32[]{:S(2)}) async-start(s32[4,1,96]{2,1,0:T(1,128)} %all_to_all.15), calls=%async_computation | async-start | bytes 4096 | tf_op jit(solution)/shard_map/all_to_all | solution.py:78
  12.3 58.3 %collective-permute-start = (bf16[12,4096]{1,0:T(8,128)(2,1)}, bf16[12,4096]{1,0:T(8,128)(2,1)S(1)}, u32[]{:S(2)}, u32[]{:S(2)}) collective-permute-start(bf16[12,4096]{1,0:T(8,128)(2,1)} %gather_fusion.1), channel_id=1, source_target_pairs={{0,4},{4,8},{8,12},{12,16},{16,20},{20,24},{24,28},{1,5},{5,9},{9,... | collective-permute-start | bytes 294920 | tf_op jit(solution)/shard_map/ppermute | solution.py:17
  17.5 54.6 %collective-permute-start.1 = (bf16[12,4096]{1,0:T(8,128)(2,1)}, bf16[12,4096]{1,0:T(8,128)(2,1)S(1)}, u32[]{:S(2)}, u32[]{:S(2)}) collective-permute-start(bf16[12,4096]{1,0:T(8,128)(2,1)} %gather_fusion.2), channel_id=1, source_target_pairs={{4,0},{8,4},{12,8},{16,12},{20,16},{24,20},{28,24},{5,1},{9,5},{13... | collective-permute-start | bytes 294920 | tf_op jit(solution)/shard_map/ppermute | solution.py:17
  20.0 46.9 %collective-permute-start.2 = (bf16[4,4096]{1,0:T(4,128)(2,1)}, bf16[4,4096]{1,0:T(4,128)(2,1)}, u32[]{:S(2)}, u32[]{:S(2)}) collective-permute-start(bf16[4,4096]{1,0:T(4,128)(2,1)} %gather_fusion.3), channel_id=1, source_target_pairs={{0,1},{1,2},{2,3},{4,5},{5,6},{6,7},{8,9},{9,10},{10,11},{12,13},{... | collective-permute-start | bytes 98312 | tf_op jit(solution)/shard_map/ppermute | solution.py:17
  23.8 44.3 %collective-permute-start.3 = (bf16[4,4096]{1,0:T(4,128)(2,1)}, bf16[4,4096]{1,0:T(4,128)(2,1)}, u32[]{:S(2)}, u32[]{:S(2)}) collective-permute-start(bf16[4,4096]{1,0:T(4,128)(2,1)} %gather_fusion.4), channel_id=1, source_target_pairs={{1,0},{2,1},{3,2},{5,4},{6,5},{7,6},{9,8},{10,9},{11,10},{13,12},{... | collective-permute-start | bytes 98312 | tf_op jit(solution)/shard_map/ppermute | solution.py:17
  26.4 51.8 %collective-permute-start.4 = (bf16[12,4096]{1,0:T(8,128)(2,1)}, bf16[12,4096]{1,0:T(8,128)(2,1)S(1)}, u32[]{:S(2)}, u32[]{:S(2)}) collective-permute-start(bf16[12,4096]{1,0:T(8,128)(2,1)} %gather_fusion.7), channel_id=1, source_target_pairs={{0,4},{4,8},{8,12},{12,16},{16,20},{20,24},{24,28},{1,5},{5,9},{9,... | collective-permute-start | bytes 294920 | tf_op jit(solution)/shard_map/ppermute | solution.py:17
  33.0 28.7 %all-to-all-start.2 = ((f32[4,1,96]{2,1,0:T(1,128)}), f32[4,1,96]{2,1,0:T(1,128)S(1)}, u32[]{:S(2)}, u32[]{:S(2)}) async-start(f32[4,1,96]{2,1,0:T(1,128)} %all_to_all.18), calls=%async_computation.2 | async-start | bytes 4096 | tf_op jit(solution)/shard_map/all_to_all | solution.py:76
  66.9 11.4 %collective-permute-start.5 = (bf16[12,4096]{1,0:T(8,128)(2,1)}, bf16[12,4096]{1,0:T(8,128)(2,1)S(1)}, u32[]{:S(2)}, u32[]{:S(2)}) collective-permute-start(bf16[12,4096]{1,0:T(8,128)(2,1)} %gather_fusion.8), channel_id=1, source_target_pairs={{4,0},{8,4},{12,8},{16,12},{20,16},{24,20},{28,24},{5,1},{9,5},{13... | collective-permute-start | bytes 294920 | tf_op jit(solution)/shard_map/ppermute | solution.py:17
  68.2 10.0 %collective-permute-start.6 = (bf16[4,4096]{1,0:T(4,128)(2,1)}, bf16[4,4096]{1,0:T(4,128)(2,1)S(1)}, u32[]{:S(2)}, u32[]{:S(2)}) collective-permute-start(bf16[4,4096]{1,0:T(4,128)(2,1)} %gather_fusion.9), channel_id=1, source_target_pairs={{0,1},{1,2},{2,3},{4,5},{5,6},{6,7},{8,9},{9,10},{10,11},{12,13},{... | collective-permute-start | bytes 98312 | tf_op jit(solution)/shard_map/ppermute | solution.py:17
  70.6 7.6 %collective-permute-start.7 = (bf16[4,4096]{1,0:T(4,128)(2,1)}, bf16[4,4096]{1,0:T(4,128)(2,1)S(1)}, u32[]{:S(2)}, u32[]{:S(2)}) collective-permute-start(bf16[4,4096]{1,0:T(4,128)(2,1)} %gather_fusion.10), channel_id=1, source_target_pairs={{1,0},{2,1},{3,2},{5,4},{6,5},{7,6},{9,8},{10,9},{11,10},{13,12},{... | collective-permute-start | bytes 98312 | tf_op jit(solution)/shard_map/ppermute | solution.py:17
  80.7 6.4 %copy-start.2 = (f32[96,64,64]{2,1,0:T(8,128)S(1)}, f32[96,64,64]{2,1,0:T(8,128)}, u32[]{:S(2)}) copy-start(f32[96,64,64]{2,1,0:T(8,128)} %copy.23) | copy-start | bytes 4718596
  87.1 2.6 %copy-start.3 = (bf16[96,64,64]{2,1,0:T(8,128)(2,1)S(1)}, bf16[96,64,64]{2,1,0:T(8,128)(2,1)}, u32[]{:S(2)}) copy-start(bf16[96,64,64]{2,1,0:T(8,128)(2,1)} %copy.17) | copy-start | bytes 2359300
  87.1 3.3 %copy-start.4 = (f32[96,64,64]{2,1,0:T(8,128)S(1)}, f32[96,64,64]{2,1,0:T(8,128)}, u32[]{:S(2)}) copy-start(f32[96,64,64]{2,1,0:T(8,128)} %copy.18) | copy-start | bytes 4718596
  87.1 3.8 %copy-start.5 = (bf16[96,64,64]{2,1,0:T(8,128)(2,1)S(1)}, bf16[96,64,64]{2,1,0:T(8,128)(2,1)}, u32[]{:S(2)}) copy-start(bf16[96,64,64]{2,1,0:T(8,128)(2,1)} %copy.21) | copy-start | bytes 2359300
  90.9 0.8 copy-start.8
  90.9 0.9 copy-start.7
  93.5 48.4 %all-to-all-start.1 = ((f32[4,96,128]{2,1,0:T(8,128)}), f32[4,96,128]{2,1,0:T(8,128)S(1)}, u32[]{:S(2)}, u32[]{:S(2)}) async-start(f32[4,96,128]{2,1,0:T(8,128)} %bitcast.18), calls=%async_computation.1 | async-start | bytes 393216 | tf_op jit(solution)/shard_map/all_to_all | solution.py:73
where the time goes:
time: 146 us
  local copies, waits for them, and re-layouts  50.3 us (34%)
  blocking collectives  42.7 us (29%)
  starting transfers between devices  33.1 us (23%)
  other arithmetic  15 us (10%)
  matrix products  3.43 us (2%)
    psum x1, blocking collectives, shards(): lax.psum(jnp.sum(energy, axis=0), ('gx', 'gy')) / math.sqrt(total_tiles)  42.7 us
    ppermute x8, starting transfers between devices, shifted(): return lax.ppermute(x, axis, pairs)  18.6 us
    all_to_all x1, starting transfers between devices, shards(): lax.all_to_all(buffer.reshape(rows_y, CAP, 2 * R), 'gy', split_axis=0, co...  5.15 us
    all_to_all x1, starting transfers between devices, shards(): lax.all_to_all(weights.reshape(rows_y, CAP), 'gy', split_axis=0, concat_a...  5.13 us
    convert_element_type x2, local copies, waits for them, and re-layouts, shards(): lrow = adjoint[tile_rows].reshape(count, BS, R).astype(jnp.float32)  5.11 us
    convert_element_type x2, local copies, waits for them, and re-layouts, shards(): urow = disp[tile_rows].reshape(count, BS, R).astype(jnp.float32)  5.09 us
    gather x2, local copies, waits for them, and re-layouts, shards(): lcol = adj_ext[tile_cols].reshape(count, BS, R)  4.29 us
    all_to_all x1, starting transfers between devices, shards(): lax.all_to_all(labels.reshape(rows_y, CAP), 'gy', split_axis=0, concat_ax...  4.21 us
  transfers between devices with their start and end apart: 11, of which 0 were waited for; matrix products, arithmetic and copies ran while one was open for 31% of the time, Pallas kernels for 0%

commit v1 on v0

v1 whole, which is shorter than its diff:
```python
import functools
import math

import jax
import jax.numpy as jnp
from jax import lax
from jax.experimental import pallas as pl
from jax.experimental.pallas import tpu as pltpu
from jax.sharding import PartitionSpec as P

BS = 64
R = 64
NREG = 32
LANES = 2 * R
HALF = BS // 2
MESH = pl.DeviceIdType.MESH
BF16 = jnp.bfloat16
F32 = jnp.float32


def loop(count, unroll, body):
    def step(i, carry):
        for k in range(unroll):
            body(i * unroll + k)
        return carry

    lax.fori_loop(0, count // unroll, step, 0)


def exchange(src, dst, send_sem, recv_sem, where):
    return pltpu.make_async_remote_copy(
        src_ref=src,
        dst_ref=dst,
        send_sem=send_sem,
        recv_sem=recv_sem,
        device_id=where,
        device_id_type=MESH,
    )


def two_terms(x):
    high = x.astype(BF16)
    low = (x - high.astype(F32)).astype(BF16)
    return jnp.concatenate([high, low], axis=0)


def rows_by_region(onehot, x):
    doubled = jnp.concatenate([onehot, onehot], axis=0)
    return lax.dot_general(
        doubled, two_terms(x), (((0,), (0,)), ((), ())), preferred_element_type=F32
    )


def kernel(
    n_gx,
    n_gy,
    rows_ref,
    cols_ref,
    density_ref,
    weight_ref,
    owner_ref,
    region_ref,
    face_x_ref,
    face_y_ref,
    disp_hbm,
    adj_hbm,
    tiles_hbm,
    filtered_ref,
    compliance_ref,
    disp_raw,
    adj_raw,
    tiles_raw,
    disp_wide,
    adj_wide,
    tiles_wide,
    local,
    ext,
    staged,
    prod,
    prod_swapped,
    onehot,
    weights,
    partial,
    energy,
    totals_out,
    totals_in,
    sums_out,
    sums_in,
    comp_out,
    comp_in,
    load_sem,
    halo_send,
    halo_recv,
    totals_send,
    totals_recv,
    sums_send,
    sums_recv,
    comp_send,
    comp_recv,
):
    count = tiles_hbm.shape[0]
    blocks = disp_hbm.shape[0]
    nix = face_x_ref.shape[0] // 2
    niy = face_y_ref.shape[0] // 2
    gx = lax.axis_index("gx")
    gy = lax.axis_index("gy")

    loads = [
        pltpu.make_async_copy(src, dst, load_sem.at[k])
        for k, (src, dst) in enumerate(
            ((disp_hbm, disp_raw), (adj_hbm, adj_raw), (tiles_hbm, tiles_raw))
        )
    ]
    for load in loads:
        load.start()

    barrier = pltpu.get_barrier_semaphore()

    @pl.loop(0, n_gx)
    def _(i):
        @pl.when(i != gx)
        def _():
            pl.semaphore_signal(barrier, inc=1, device_id=(i, gy), device_id_type=MESH)

    @pl.loop(0, n_gy)
    def _(j):
        @pl.when(j != gy)
        def _():
            pl.semaphore_signal(barrier, inc=1, device_id=(gx, j), device_id_type=MESH)

    def widen(raw, wide, height):
        def body(c):
            chunk = raw[:, pl.ds(pl.multiple_of(c * LANES, LANES), LANES)]
            wide[pl.ds(pl.multiple_of(c * height, 8), height), :] = chunk.astype(F32)

        loop(HALF, 4, body)

    low_lanes = lax.broadcasted_iota(jnp.int32, (HALF, LANES), 1) < R

    loads[0].wait()
    widen(disp_raw, disp_wide, blocks)
    loads[1].wait()
    widen(adj_raw, adj_wide, blocks)

    def local_block(b):
        u = disp_wide[pl.ds(b, HALF, stride=blocks), :]
        a = adj_wide[pl.ds(b, HALF, stride=blocks), :]
        even = jnp.where(low_lanes, a, pltpu.roll(u, R, 1))
        odd = jnp.where(low_lanes, pltpu.roll(a, R, 1), u)
        block = jnp.concatenate([even, odd], axis=0).astype(BF16)
        local[b] = block
        ext[b] = block

    loop(blocks, 4, local_block)

    def stage(faces, first, number):
        def body(k):
            staged[first + k] = local[faces[k]]

        loop(number, 4, body)

    stage(face_x_ref, 0, 2 * nix)
    stage(face_y_ref, 2 * nix, 2 * niy)

    pl.semaphore_wait(barrier, n_gx + n_gy - 2)

    first = blocks
    plans = (
        (0, first, nix, gx < n_gx - 1, (gx + 1, gy), gx > 0),
        (nix, first + nix, nix, gx > 0, (gx - 1, gy), gx < n_gx - 1),
        (2 * nix, first + 2 * nix, niy, gy < n_gy - 1, (gx, gy + 1), gy > 0),
        (2 * nix + niy, first + 2 * nix + niy, niy, gy > 0, (gx, gy - 1), gy < n_gy - 1),
    )

    def halo(k):
        at, to, number, _, where, _ = plans[k]
        return exchange(
            staged.at[pl.ds(at, number)],
            ext.at[pl.ds(to, number)],
            halo_send.at[k],
            halo_recv.at[k],
            where,
        )

    for k, (_, to, number, has_target, _, has_source) in enumerate(plans):

        @pl.when(has_target)
        def _(k=k):
            halo(k).start()

        @pl.when(jnp.logical_not(has_source))
        def _(to=to, number=number):
            ext[pl.ds(to, number)] = jnp.zeros((number, BS, LANES), BF16)

    regions = n_gy * NREG
    key_lane = lax.broadcasted_iota(jnp.int32, (1, regions), 1)

    def key_row(t):
        key = owner_ref[t] * NREG + region_ref[t]
        onehot[pl.ds(t, 1), :] = (key_lane == key).astype(F32)
        weights[pl.ds(t, 1), :] = jnp.full((1, LANES), weight_ref[t], F32)

    loop(count, 4, key_row)
    hot = onehot[...].astype(BF16)
    totals_out[...] = rows_by_region(hot, weights[...]).reshape(n_gy, NREG, LANES)
    totals_in[gy] = totals_out[gy]

    def totals_copy(j, slot):
        return exchange(
            totals_out.at[j], totals_in.at[slot], totals_send.at[j], totals_recv.at[slot], (gx, j)
        )

    def sums_copy(j, slot):
        return exchange(
            sums_out.at[j], sums_in.at[slot], sums_send.at[j], sums_recv.at[slot], (gx, j)
        )

    def comp_copy(i, slot):
        return exchange(comp_out, comp_in.at[slot], comp_send.at[i], comp_recv.at[slot], (i, gy))

    def others(size, me, body):
        @pl.loop(0, size)
        def _(i):
            @pl.when(i != me)
            def _():
                body(i)

    others(n_gy, gy, lambda j: totals_copy(j, gy).start())

    loads[2].wait()
    widen(tiles_raw, tiles_wide, count)

    def product(t):
        pair = tiles_wide[pl.ds(t, HALF, stride=count), :]
        even = pair[:, :BS]
        odd = pltpu.roll(pair, BS, 1)[:, :BS]
        tile = jnp.concatenate([even, odd], axis=0).astype(BF16)
        block = local[rows_ref[t]]
        result = lax.dot_general(
            tile, block, (((0,), (0,)), ((), ())), preferred_element_type=F32
        )
        at = pl.ds(pl.multiple_of(t * BS, BS), BS)
        prod[at, :] = result
        prod_swapped[at, :] = pltpu.roll(result, R, 1)

    loop(count, 4, product)

    others(n_gy, gy, lambda j: totals_copy(j, j).wait_recv())
    total = jnp.zeros((NREG, LANES), F32)
    for j in range(n_gy):
        total = total + totals_in[j]
    scale = 1.0 / jnp.maximum(total, 1.0)

    for k, (_, _, _, _, _, has_source) in enumerate(plans):

        @pl.when(has_source)
        def _(k=k):
            halo(k).wait_recv()

    low8 = lax.broadcasted_iota(jnp.int32, (8, LANES), 1) < R

    def fold(x):
        parts = [x[8 * k : 8 * k + 8, :] for k in range(HALF // 8)]
        return (parts[0] + parts[1]) + (parts[2] + parts[3])

    def element(t):
        base = t * BS
        block = ext[cols_ref[t]]
        even = block[0:HALF, :].astype(F32)
        odd = block[HALF:BS, :].astype(F32)
        at_even = pl.ds(base, HALF, stride=2)
        at_odd = pl.ds(base + 1, HALF, stride=2)
        straight = fold(prod[at_even, :] * even + prod[at_odd, :] * odd)
        crossed = fold(prod_swapped[at_even, :] * even + prod_swapped[at_odd, :] * odd)
        cross = crossed + pltpu.roll(crossed, R, 1)
        strain = straight * (1.0 / math.sqrt(BS))
        rho = density_ref[t]
        sens = cross * (-(3.0 * rho * rho / (2.0 * math.sqrt(BS))))
        at = pl.ds(pl.multiple_of(t * 8, 8), 8)
        partial[at, :] = weight_ref[t] * jnp.where(low8, sens, strain)
        return strain

    unroll = 4

    def elements(i, total_energy):
        for k in range(unroll):
            total_energy = total_energy + element(i * unroll + k)
        return total_energy

    comp = lax.fori_loop(0, count // unroll, elements, jnp.zeros((8, LANES), F32))

    payload = partial[pl.ds(0, count, stride=8), :]
    for s in range(1, 8):
        payload = payload + partial[pl.ds(s, count, stride=8), :]
    sums_out[:, 0:NREG, :] = rows_by_region(hot, payload).reshape(n_gy, NREG, LANES)
    for j in range(n_gy):
        sums_out[j, NREG : NREG + 8, :] = comp
    sums_in[gy] = sums_out[gy]
    others(n_gy, gy, lambda j: sums_copy(j, gy).start())
    others(n_gy, gy, lambda j: sums_copy(j, j).wait_recv())
    gathered = sums_in[0]
    for j in range(1, n_gy):
        gathered = gathered + sums_in[j]
    comp_out[...] = gathered[NREG : NREG + 8, :]
    comp_in[gx] = comp_out[...]
    others(n_gx, gx, lambda i: comp_copy(i, gx).start())
    filtered_ref[...] = gathered[0:NREG, :] * scale

    for k, (_, _, _, has_target, _, _) in enumerate(plans):

        @pl.when(has_target)
        def _(k=k):
            halo(k).wait_send()

    others(n_gy, gy, lambda j: totals_copy(j, gy).wait_send())
    others(n_gy, gy, lambda j: sums_copy(j, gy).wait_send())

    others(n_gx, gx, lambda i: comp_copy(i, i).wait_recv())
    everything = lax.fori_loop(
        0, n_gx, lambda i, acc: acc + comp_in[i], jnp.zeros((8, LANES), F32)
    )
    line = jnp.sum(everything, axis=0, keepdims=True) / math.sqrt(count * n_gx * n_gy)
    compliance_ref[...] = pltpu.roll(jnp.broadcast_to(line, (8, LANES)), R, 1)[0:1, :]
    others(n_gx, gx, lambda i: comp_copy(i, gx).wait_send())


def shards(n_gx, n_gy, *args):
    (
        disp,
        adjoint,
        tiles,
        tile_rows,
        tile_cols,
        density,
        filter_weight,
        owner,
        region,
        face_x,
        face_y,
    ) = args
    count = tiles.shape[0]
    blocks = disp.shape[0]
    faces = face_x.shape[2] * 2 + face_y.shape[2] * 2
    smem = pl.BlockSpec(memory_space=pltpu.SMEM)
    hbm = pl.BlockSpec(memory_space=pl.ANY)
    vmem = pl.BlockSpec(memory_space=pltpu.VMEM)
    dma = pltpu.SemaphoreType.DMA
    filtered, compliance = pl.pallas_call(
        functools.partial(kernel, n_gx, n_gy),
        out_shape=(
            jax.ShapeDtypeStruct((NREG, LANES), F32),
            jax.ShapeDtypeStruct((1, LANES), F32),
        ),
        in_specs=[smem] * 8 + [hbm] * 3,
        out_specs=(vmem, vmem),
        scratch_shapes=[
            pltpu.VMEM((blocks, BS * R), BF16),
            pltpu.VMEM((blocks, BS * R), BF16),
            pltpu.VMEM((count, BS * BS), BF16),
            pltpu.VMEM((HALF * blocks, LANES), F32),
            pltpu.VMEM((HALF * blocks, LANES), F32),
            pltpu.VMEM((HALF * count, LANES), F32),
            pltpu.VMEM((blocks, BS, LANES), BF16),
            pltpu.VMEM((blocks + faces, BS, LANES), BF16),
            pltpu.VMEM((faces, BS, LANES), BF16),
            pltpu.VMEM((count * BS, LANES), F32),
            pltpu.VMEM((count * BS, LANES), F32),
            pltpu.VMEM((count, n_gy * NREG), F32),
            pltpu.VMEM((count, LANES), F32),
            pltpu.VMEM((count * 8, LANES), F32),
            pltpu.VMEM((8, LANES), F32),
            pltpu.VMEM((n_gy, NREG, LANES), F32),
            pltpu.VMEM((n_gy, NREG, LANES), F32),
            pltpu.VMEM((n_gy, NREG + 8, LANES), F32),
            pltpu.VMEM((n_gy, NREG + 8, LANES), F32),
            pltpu.VMEM((8, LANES), F32),
            pltpu.VMEM((n_gx, 8, LANES), F32),
            dma((3,)),
            dma((4,)),
            dma((4,)),
            dma((n_gy,)),
            dma((n_gy,)),
            dma((n_gy,)),
            dma((n_gy,)),
            dma((n_gx,)),
            dma((n_gx,)),
        ],
        compiler_params=pltpu.CompilerParams(
            collective_id=0, has_side_effects=True, vmem_limit_bytes=40 * 2**20
        ),
        name="sensitivities",
    )(
        tile_rows,
        tile_cols,
        density,
        filter_weight,
        owner.reshape(-1),
        region,
        face_x.reshape(-1),
        face_y.reshape(-1),
        disp,
        adjoint,
        tiles,
    )
    return filtered, compliance[0, :R]


def solution(mesh):
    placed = (
        P(("gx", "gy"), None),
        P(("gx", "gy"), None),
        P(("gx", "gy"), None),
        P(("gx", "gy")),
        P(("gx", "gy")),
        P(("gx", "gy")),
        P(("gx", "gy")),
        P(("gx", "gy"), None),
        P(("gx", "gy")),
        P(("gx", "gy"), None, None),
        P(("gx", "gy"), None, None),
    )
    return jax.shard_map(
        functools.partial(shards, mesh.shape["gx"], mesh.shape["gy"]),
        mesh=mesh,
        in_specs=placed,
        out_specs=(P(("gx", "gy"), None), P()),
        check_vma=False,
    )
```

time: 146 us -> 33.9 us (0.23)
  local copies, waits for them, and re-layouts: 50.3 us -> 5.76 us
  blocking collectives: 42.7 us -> 0 us
  starting transfers between devices: 33.1 us -> 0 us
  Pallas kernels: 0 us -> 27.2 us
  other arithmetic: 15 us -> 0 us
  matrix products: 3.43 us -> 0 us
    psum x1 -> x0, blocking collectives: 42.7 us -> none  [shards(): lax.psum(jnp.sum(energy, axis=0), ('gx', 'gy')) / math.sqrt(total_tiles)]
    pallas_call x0 -> x1, Pallas kernels: none -> 27.2 us  [shards(): pl.pallas_call(functools.partial(kernel, n_gx, n_gy), out_shape=(jax.Shap...]
    gather x14 -> x0, local copies, waits for them, and re-layouts: 20.7 us -> none  [the longest x2 4.29 us: shards(): lcol = adj_ext[tile_cols].reshape(count, BS, R)]
    ppermute x8 -> x0, starting transfers between devices: 18.6 us -> none  [shifted(): return lax.ppermute(x, axis, pairs)]
    all_to_all x3 -> x0, starting transfers between devices: 14.5 us -> none  [the longest x1 5.15 us: shards(): lax.all_to_all(buffer.reshape(rows_y, CAP, 2 * R), 'gy', split_axis=0, co...]
    convert_element_type x4 -> x0, local copies, waits for them, and re-layouts: 10.2 us -> none  [the longest x2 5.11 us: shards(): lrow = adjoint[tile_rows].reshape(count, BS, R).astype(jnp.float32)]
    reshape x4 -> x2, local copies, waits for them, and re-layouts: 10.4 us -> 0.16 us  [the longest x1 0.08 us: shards(): face_y.reshape(-1)]
    scatter-add x2 -> x0, other arithmetic: 6.89 us -> none  [the longest x1 3.87 us: shards(): jax.ops.segment_sum(got_weights.reshape(-1), flat_labels, NREG + 1)[:NREG]]
  transfers between devices with their start and end apart: 11 -> 0, of which waited for: 0 -> 0; matrix products, arithmetic and copies ran while one was open for 31% -> 0% of each run, Pallas kernels for 0% -> 0%
where the time goes in v1:
time: 33.9 us; the launch traced here: 33.6 us
  Pallas kernels  27.2 us (80%)
  local copies, waits for them, and re-layouts  5.76 us (17%)
  between operations  0.67 us (2%)
    pallas_call x1, Pallas kernels, shards(): pl.pallas_call(functools.partial(kernel, n_gx, n_gy), out_shape=(jax.Shap...  27.2 us
    unnamed x23, local copies, waits for them, and re-layouts  5.09 us

profile of v1, /device:TPU:0, one launch (start us, length us, event | category | flops | bytes accessed | tf_op | source)
XLA Modules:
  0.0 33.6 jit_solution(8880129915543569842)
XLA Ops:
  0.6 0.0 copy-start.9
  0.6 0.0 copy-start.10
  0.7 0.7 %copy-done.9 = s32[1,2,12]{2,1,0:T(2,128)S(1)} copy-done((s32[1,2,12]{2,1,0:T(2,128)S(1)}, s32[1,2,12]{2,1,0:T(2,128)}, u32[]{:S(2)}) %copy-start.9) | copy-done | bytes 120
  1.3 0.0 copy-start.6
  1.3 0.0 copy-start.7
  1.3 0.0 copy-start.8
  1.3 0.1 reshape.14.face_x_ref
  1.4 0.0 copy-done.10
  1.4 0.0 copy-start.3
  1.4 0.0 copy-start.4
  1.4 0.0 copy-start.5
  1.4 0.1 reshape.15.face_y_ref
  1.5 0.5 %copy-done.6 = f32[96]{0:T(128)S(1)} copy-done((f32[96]{0:T(128)S(1)}, f32[96]{0:T(128)}, u32[]{:S(2)}) %copy-start.6) | copy-done | bytes 408
  2.0 0.0 copy-done.7
  2.0 0.0 copy-done.8
  2.0 0.1 copy-done.3
  2.1 0.0 copy-done.4
  2.1 0.0 copy-done.5
  2.1 1.1 %copy-done = bf16[96,4096]{1,0:T(8,128)(2,1)S(1)} copy-done((bf16[96,4096]{1,0:T(8,128)(2,1)S(1)}, bf16[96,4096]{1,0:T(8,128)(2,1)}, u32[]{:S(2)}) %copy-start) | copy-done | bytes 786456
  3.2 1.0 %copy-done.1 = bf16[64,4096]{1,0:T(8,128)(2,1)S(1)} copy-done((bf16[64,4096]{1,0:T(8,128)(2,1)S(1)}, bf16[64,4096]{1,0:T(8,128)(2,1)}, u32[]{:S(2)}) %copy-start.1) | copy-done | bytes 524312
  4.3 1.0 %copy-done.2 = bf16[64,4096]{1,0:T(8,128)(2,1)S(1)} copy-done((bf16[64,4096]{1,0:T(8,128)(2,1)S(1)}, bf16[64,4096]{1,0:T(8,128)(2,1)}, u32[]{:S(2)}) %copy-start.2) | copy-done | bytes 524312
  5.3 27.2 %sensitivities.1 = (f32[32,128]{1,0:T(8,128)S(1)}, f32[1,128]{1,0:T(1,128)S(1)}) custom-call(s32[96]{0:T(128)S(1)} %copy-done.3, s32[96]{0:T(128)S(1)} %copy-done.4, f32[96]{0:T(128)S(1)} %copy-done.5, f32[96]{0:T(128)S(1)} %copy-done.6, s32[96]{0:T(128)S(1)} %bitcast.3, s32[96]{0:T(128)S(1)} %copy-done.8, s32[24]{0:T(128)S(1)} %reshape.14.face_x_ref, ...), custom_call_target="tpu_custom_call" | custom-call | tf_op jit(solution)/shard_map/sensitivities/pallas_call | solution.py:348
  32.5 0.5 %slice_bitcast_fusion = f32[64]{0:T(128)} fusion(f32[1,128]{1,0:T(1,128)S(1)} %get-tuple-element.5), kind=kLoop, calls=%fused_computation | loop fusion | bytes 512 | tf_op jit(solution)/shard_map/squeeze | solution.py:405
  33.0 0.6 %copy.14 = f32[32,128]{1,0:T(8,128)} copy(f32[32,128]{1,0:T(8,128)S(1)} %get-tuple-element.8) | data formatting | bytes 32768
  (3 shorter events, 0.0 us)
Async XLA Ops:
  0.6 0.7 %copy-start.9 = (s32[1,2,12]{2,1,0:T(2,128)S(1)}, s32[1,2,12]{2,1,0:T(2,128)}, u32[]{:S(2)}) copy-start(s32[1,2,12]{2,1,0:T(2,128)} %param.20) | copy-start | bytes 292
  0.6 0.8 %copy-start.10 = (s32[1,2,4]{2,1,0:T(2,128)S(1)}, s32[1,2,4]{2,1,0:T(2,128)}, u32[]{:S(2)}) copy-start(s32[1,2,4]{2,1,0:T(2,128)} %param.21) | copy-start | bytes 100
  1.3 0.7 %copy-start.6 = (f32[96]{0:T(128)S(1)}, f32[96]{0:T(128)}, u32[]{:S(2)}) copy-start(f32[96]{0:T(128)} %weight_ref.1) | copy-start | bytes 1156
  1.3 0.7 %copy-start.7 = (s32[96,1]{0,1:T(1,128)S(1)}, s32[96,1]{0,1:T(1,128)}, u32[]{:S(2)}) copy-start(s32[96,1]{0,1:T(1,128)} %param.18) | copy-start | bytes 1156
  1.3 0.7 %copy-start.8 = (s32[96]{0:T(128)S(1)}, s32[96]{0:T(128)}, u32[]{:S(2)}) copy-start(s32[96]{0:T(128)} %region_ref.1) | copy-start | bytes 1156
  1.4 0.7 %copy-start.3 = (s32[96]{0:T(128)S(1)}, s32[96]{0:T(128)}, u32[]{:S(2)}) copy-start(s32[96]{0:T(128)} %rows_ref.1) | copy-start | bytes 1156
  1.4 0.7 %copy-start.4 = (s32[96]{0:T(128)S(1)}, s32[96]{0:T(128)}, u32[]{:S(2)}) copy-start(s32[96]{0:T(128)} %cols_ref.1) | copy-start | bytes 1156
  1.4 0.7 %copy-start.5 = (f32[96]{0:T(128)S(1)}, f32[96]{0:T(128)}, u32[]{:S(2)}) copy-start(f32[96]{0:T(128)} %density_ref.1) | copy-start | bytes 1156
  2.1 1.1 %copy-start = (bf16[96,4096]{1,0:T(8,128)(2,1)S(1)}, bf16[96,4096]{1,0:T(8,128)(2,1)}, u32[]{:S(2)}) copy-start(bf16[96,4096]{1,0:T(8,128)(2,1)} %tiles_hbm.1) | copy-start | bytes 2359300
  3.2 1.0 %copy-start.1 = (bf16[64,4096]{1,0:T(8,128)(2,1)S(1)}, bf16[64,4096]{1,0:T(8,128)(2,1)}, u32[]{:S(2)}) copy-start(bf16[64,4096]{1,0:T(8,128)(2,1)} %disp_hbm.1) | copy-start | bytes 1572868
  4.3 1.0 %copy-start.2 = (bf16[64,4096]{1,0:T(8,128)(2,1)S(1)}, bf16[64,4096]{1,0:T(8,128)(2,1)}, u32[]{:S(2)}) copy-start(bf16[64,4096]{1,0:T(8,128)(2,1)} %adj_hbm.1) | copy-start | bytes 1572868

commit v2 on v1

--- a/solution.py
+++ b/solution.py
@@ -16,6 +16,7 @@
 MESH = pl.DeviceIdType.MESH
 BF16 = jnp.bfloat16
 F32 = jnp.float32
+I32 = jnp.int32
 
 
 def loop(count, unroll, body):
@@ -54,6 +55,19 @@
 def kernel(
     n_gx,
     n_gy,
+    rows_hbm,
+    cols_hbm,
+    density_hbm,
+    weight_hbm,
+    owner_hbm,
+    region_hbm,
+    face_x_hbm,
+    face_y_hbm,
+    disp_hbm,
+    adj_hbm,
+    tiles_hbm,
+    filtered_ref,
+    compliance_ref,
     rows_ref,
     cols_ref,
     density_ref,
@@ -62,11 +76,6 @@
     region_ref,
     face_x_ref,
     face_y_ref,
-    disp_hbm,
-    adj_hbm,
-    tiles_hbm,
-    filtered_ref,
-    compliance_ref,
     disp_raw,
     adj_raw,
     tiles_raw,
@@ -97,13 +106,37 @@
     sums_recv,
     comp_send,
     comp_recv,
+    scalar_sem,
+    known_x,
+    known_y,
 ):
     count = tiles_hbm.shape[0]
     blocks = disp_hbm.shape[0]
-    nix = face_x_ref.shape[0] // 2
-    niy = face_y_ref.shape[0] // 2
+    nix = face_x_ref.shape[2]
+    niy = face_y_ref.shape[2]
     gx = lax.axis_index("gx")
     gy = lax.axis_index("gy")
+
+    barrier = pltpu.get_barrier_semaphore()
+
+    def each_way(distance, body):
+        for side, (place, size, where) in enumerate(
+            ((gx, n_gx, lambda d: (gx + d, gy)), (gy, n_gy, lambda d: (gx, gy + d)))
+        ):
+            if distance < size:
+
+                @pl.when(place + distance < size)
+                def _(side=side, where=where):
+                    body(side, 0, where(distance))
+
+                @pl.when(place >= distance)
+                def _(side=side, where=where):
+                    body(side, 1, where(-distance))
+
+    def greet(side, way, where):
+        pl.semaphore_signal(barrier, inc=1, device_id=where, device_id_type=MESH)
+
+    each_way(1, greet)
 
     loads = [
         pltpu.make_async_copy(src, dst, load_sem.at[k])
@@ -111,22 +144,41 @@
             ((disp_hbm, disp_raw), (adj_hbm, adj_raw), (tiles_hbm, tiles_raw))
         )
     ]
-    for load in loads:
+    scalar_loads = [
+        pltpu.make_async_copy(src, dst, scalar_sem.at[k])
+        for k, (src, dst) in enumerate(
+            (
+                (face_x_hbm, face_x_ref),
+                (face_y_hbm, face_y_ref),
+                (rows_hbm, rows_ref),
+                (cols_hbm, cols_ref),
+                (density_hbm, density_ref),
+                (weight_hbm, weight_ref),
+                (owner_hbm, owner_ref),
+                (region_hbm, region_ref),
+            )
+        )
+    ]
+    for load in loads[:2] + scalar_loads + loads[2:]:
         load.start()
 
-    barrier = pltpu.get_barrier_semaphore()
-
-    @pl.loop(0, n_gx)
-    def _(i):
-        @pl.when(i != gx)
-        def _():
-            pl.semaphore_signal(barrier, inc=1, device_id=(i, gy), device_id_type=MESH)
-
-    @pl.loop(0, n_gy)
-    def _(j):
-        @pl.when(j != gy)
-        def _():
-            pl.semaphore_signal(barrier, inc=1, device_id=(gx, j), device_id_type=MESH)
+    def learn_start(step):
+        def body(side, way, where):
+            known = known_x if side == 0 else known_y
+            pl.semaphore_signal(
+                known.at[step, way], inc=1, device_id=where, device_id_type=MESH
+            )
+
+        each_way(2**step, body)
+
+    def learn_finish(step):
+        def body(side, way, where):
+            known = known_x if side == 0 else known_y
+            pl.semaphore_wait(known.at[step, 1 - way], 1)
+
+        each_way(2**step, body)
+
+    steps = (max(n_gx, n_gy) - 1).bit_length()
 
     def widen(raw, wide, height):
         def body(c):
@@ -142,27 +194,30 @@
     loads[1].wait()
     widen(adj_raw, adj_wide, blocks)
 
-    def local_block(b):
+    def parts(b):
         u = disp_wide[pl.ds(b, HALF, stride=blocks), :]
         a = adj_wide[pl.ds(b, HALF, stride=blocks), :]
-        even = jnp.where(low_lanes, a, pltpu.roll(u, R, 1))
-        odd = jnp.where(low_lanes, pltpu.roll(a, R, 1), u)
+        u_turned = pltpu.roll(u, R, 1)
+        a_turned = pltpu.roll(a, R, 1)
+        even = jnp.where(low_lanes, a, u_turned)
+        odd = jnp.where(low_lanes, a_turned, u)
+        even_swapped = jnp.where(low_lanes, u, a_turned)
+        odd_swapped = jnp.where(low_lanes, u_turned, a)
         block = jnp.concatenate([even, odd], axis=0).astype(BF16)
-        local[b] = block
+        swapped = jnp.concatenate([even_swapped, odd_swapped], axis=0).astype(BF16)
+        return block, swapped
+
+    def local_block(b):
+        block, swapped = parts(b)
+        local[b, :, 0:LANES] = block
+        local[b, :, LANES : 2 * LANES] = swapped
         ext[b] = block
 
-    loop(blocks, 4, local_block)
-
-    def stage(faces, first, number):
+    def stage(faces, way, at, number):
         def body(k):
-            staged[first + k] = local[faces[k]]
+            staged[at + k] = parts(faces[0, way, k])[0]
 
         loop(number, 4, body)
-
-    stage(face_x_ref, 0, 2 * nix)
-    stage(face_y_ref, 2 * nix, 2 * niy)
-
-    pl.semaphore_wait(barrier, n_gx + n_gy - 2)
 
     first = blocks
     plans = (
@@ -182,7 +237,18 @@
             where,
         )
 
-    for k, (_, to, number, has_target, _, has_source) in enumerate(plans):
+    for load in scalar_loads[:2]:
+        load.wait()
+    for k, (at, to, number, has_target, _, has_source) in enumerate(plans):
+        stage(face_x_ref if k < 2 else face_y_ref, k % 2, at, number)
+        if k == 0:
+            neighbours = (
+                (gx > 0).astype(jnp.int32)
+                + (gx < n_gx - 1).astype(jnp.int32)
+                + (gy > 0).astype(jnp.int32)
+                + (gy < n_gy - 1).astype(jnp.int32)
+            )
+            pl.semaphore_wait(barrier, neighbours)
 
         @pl.when(has_target)
         def _(k=k):
@@ -191,6 +257,16 @@
         @pl.when(jnp.logical_not(has_source))
         def _(to=to, number=number):
             ext[pl.ds(to, number)] = jnp.zeros((number, BS, LANES), BF16)
+
+    learn_start(0)
+    loop(blocks, 4, local_block)
+    learn_finish(0)
+    for step in range(1, steps):
+        learn_start(step)
+        if step < steps - 1:
+            learn_finish(step)
+    for load in scalar_loads[2:]:
+        load.wait()
 
     regions = n_gy * NREG
     key_lane = lax.broadcasted_iota(jnp.int32, (1, regions), 1)
@@ -225,25 +301,30 @@
             def _():
                 body(i)
 
-    others(n_gy, gy, lambda j: totals_copy(j, gy).start())
-
     loads[2].wait()
     widen(tiles_raw, tiles_wide, count)
 
-    def product(t):
-        pair = tiles_wide[pl.ds(t, HALF, stride=count), :]
-        even = pair[:, :BS]
-        odd = pltpu.roll(pair, BS, 1)[:, :BS]
-        tile = jnp.concatenate([even, odd], axis=0).astype(BF16)
-        block = local[rows_ref[t]]
-        result = lax.dot_general(
-            tile, block, (((0,), (0,)), ((), ())), preferred_element_type=F32
-        )
-        at = pl.ds(pl.multiple_of(t * BS, BS), BS)
-        prod[at, :] = result
-        prod_swapped[at, :] = pltpu.roll(result, R, 1)
-
-    loop(count, 4, product)
+    def products(i):
+        t = 2 * i
+        one = tiles_wide[pl.ds(t, HALF, stride=count), :]
+        two = tiles_wide[pl.ds(t + 1, HALF, stride=count), :]
+        even = jnp.where(low_lanes, one, pltpu.roll(two, BS, 1))
+        odd = jnp.where(low_lanes, pltpu.roll(one, BS, 1), two)
+        turned = jnp.concatenate([even, odd], axis=0).astype(BF16).T
+        for k in range(2):
+            result = jnp.dot(
+                turned[k * BS : (k + 1) * BS, :],
+                local[rows_ref[t + k]],
+                preferred_element_type=F32,
+            )
+            at = pl.ds(pl.multiple_of((t + k) * BS, BS), BS)
+            prod[at, :] = result[:, 0:LANES]
+            prod_swapped[at, :] = result[:, LANES : 2 * LANES]
+
+    loop(count // 2, 2, products)
+    if steps > 1:
+        learn_finish(steps - 1)
+    others(n_gy, gy, lambda j: totals_copy(j, gy).start())
 
     others(n_gy, gy, lambda j: totals_copy(j, j).wait_recv())
     total = jnp.zeros((NREG, LANES), F32)
@@ -341,8 +422,8 @@
     count = tiles.shape[0]
     blocks = disp.shape[0]
     faces = face_x.shape[2] * 2 + face_y.shape[2] * 2
-    smem = pl.BlockSpec(memory_space=pltpu.SMEM)
-    hbm = pl.BlockSpec(memory_space=pl.ANY)
+    hbm = pl.BlockSpec(memory_space=pltpu.HBM)
+    steps = (max(n_gx, n_gy) - 1).bit_length()
     vmem = pl.BlockSpec(memory_space=pltpu.VMEM)
     dma = pltpu.SemaphoreType.DMA
     filtered, compliance = pl.pallas_call(
@@ -351,16 +432,19 @@
             jax.ShapeDtypeStruct((NREG, LANES), F32),
             jax.ShapeDtypeStruct((1, LANES), F32),
         ),
-        in_specs=[smem] * 8 + [hbm] * 3,
+        in_specs=[hbm] * 11,
         out_specs=(vmem, vmem),
         scratch_shapes=[
+            *(pltpu.SMEM((count,), kind) for kind in (I32, I32, F32, F32, I32, I32)),
+            pltpu.SMEM(face_x.shape, I32),
+            pltpu.SMEM(face_y.shape, I32),
             pltpu.VMEM((blocks, BS * R), BF16),
             pltpu.VMEM((blocks, BS * R), BF16),
             pltpu.VMEM((count, BS * BS), BF16),
             pltpu.VMEM((HALF * blocks, LANES), F32),
             pltpu.VMEM((HALF * blocks, LANES), F32),
             pltpu.VMEM((HALF * count, LANES), F32),
-            pltpu.VMEM((blocks, BS, LANES), BF16),
+            pltpu.VMEM((blocks, BS, 2 * LANES), BF16),
             pltpu.VMEM((blocks + faces, BS, LANES), BF16),
             pltpu.VMEM((faces, BS, LANES), BF16),
             pltpu.VMEM((count * BS, LANES), F32),
@@ -384,9 +468,12 @@
             dma((n_gy,)),
             dma((n_gx,)),
             dma((n_gx,)),
+            dma((8,)),
+            pltpu.SemaphoreType.REGULAR((steps, 2)),
+            pltpu.SemaphoreType.REGULAR((steps, 2)),
         ],
         compiler_params=pltpu.CompilerParams(
-            collective_id=0, has_side_effects=True, vmem_limit_bytes=40 * 2**20
+            collective_id=0, has_side_effects=True, vmem_limit_bytes=60 * 2**20
         ),
         name="sensitivities",
     )(
@@ -396,8 +483,8 @@
         filter_weight,
         owner.reshape(-1),
         region,
-        face_x.reshape(-1),
-        face_y.reshape(-1),
+        face_x,
+        face_y,
         disp,
         adjoint,
         tiles,

time: 33.9 us -> 35.7 us (1.053)
  Pallas kernels: 27.2 us -> 32.3 us
  local copies, waits for them, and re-layouts: 5.76 us -> 2.49 us
    pallas_call x1, Pallas kernels: 27.2 us -> 32.3 us  [shards(): pl.pallas_call(functools.partial(kernel, n_gx, n_gy), out_shape=(jax.Shap...]
    unnamed x23 -> x3, local copies, waits for them, and re-layouts: 5.09 us -> 1.98 us
where the time goes in v2:
time: 35.7 us; the launch traced here: 35.5 us
  Pallas kernels  32.3 us (90%)
  local copies, waits for them, and re-layouts  2.49 us (7%)
  between operations  0.65 us (2%)
    pallas_call x1, Pallas kernels, shards(): pl.pallas_call(functools.partial(kernel, n_gx, n_gy), out_shape=(jax.Shap...  32.3 us
    unnamed x3, local copies, waits for them, and re-layouts  1.98 us

profile of v2, /device:TPU:0, one launch (start us, length us, event | category | flops | bytes accessed | tf_op | source)
XLA Modules:
  0.0 35.5 jit_solution(18370800189339403632)
XLA Ops:
  0.6 32.3 %sensitivities.1 = (f32[32,128]{1,0:T(8,128)}, f32[1,128]{1,0:T(1,128)}) custom-call(s32[96]{0:T(128)} %rows_hbm.1, s32[96]{0:T(128)} %cols_hbm.1, f32[96]{0:T(128)} %density_hbm.1, f32[96]{0:T(128)} %weight_hbm.1, s32[96]{0:T(128)} %bitcast.3, s32[96]{0:T(128)} %region_hbm.1, s32[1,2,12]{2,1,0:T(2,128)} %face_x_hbm.1, s32[1,2,4]{2,1,0:T(2,128)} %face_y_hbm.1, ...), custom_call_target="tpu_custom_call" | custom-call | tf_op jit(solution)/shard_map/sensitivities/pallas_call | solution.py:429
  33.0 0.0 copy-start
  33.0 0.7 %copy-done = f32[1,128]{1,0:T(1,128)S(1)} copy-done((f32[1,128]{1,0:T(1,128)S(1)}, f32[1,128]{1,0:T(1,128)}, u32[]{:S(2)}) %copy-start) | copy-done | bytes 536
  33.6 0.5 %slice_bitcast_fusion = f32[64]{0:T(128)} fusion(f32[1,128]{1,0:T(1,128)S(1)} %copy-done), kind=kLoop, calls=%fused_computation | loop fusion | bytes 512 | tf_op jit(solution)/shard_map/squeeze | solution.py:492
  34.1 1.3 %copy.14 = f32[32,128]{1,0:T(8,128)} copy(f32[32,128]{1,0:T(8,128)} %get-tuple-element.8) | data formatting | bytes 32768
Async XLA Ops:
  33.0 0.7 %copy-start = (f32[1,128]{1,0:T(1,128)S(1)}, f32[1,128]{1,0:T(1,128)}, u32[]{:S(2)}) copy-start(f32[1,128]{1,0:T(1,128)} %get-tuple-element.5) | copy-start | bytes 1540

commit v3 on v2

--- a/solution.py
+++ b/solution.py
@@ -183,7 +183,7 @@
     def widen(raw, wide, height):
         def body(c):
             chunk = raw[:, pl.ds(pl.multiple_of(c * LANES, LANES), LANES)]
-            wide[pl.ds(pl.multiple_of(c * height, 8), height), :] = chunk.astype(F32)
+            wide[pl.ds(c * (height + 1), height), :] = chunk.astype(F32)
 
         loop(HALF, 4, body)
 
@@ -195,8 +195,8 @@
     widen(adj_raw, adj_wide, blocks)
 
     def parts(b):
-        u = disp_wide[pl.ds(b, HALF, stride=blocks), :]
-        a = adj_wide[pl.ds(b, HALF, stride=blocks), :]
+        u = disp_wide[pl.ds(b, HALF, stride=blocks + 1), :]
+        a = adj_wide[pl.ds(b, HALF, stride=blocks + 1), :]
         u_turned = pltpu.roll(u, R, 1)
         a_turned = pltpu.roll(a, R, 1)
         even = jnp.where(low_lanes, a, u_turned)
@@ -306,8 +306,8 @@
 
     def products(i):
         t = 2 * i
-        one = tiles_wide[pl.ds(t, HALF, stride=count), :]
-        two = tiles_wide[pl.ds(t + 1, HALF, stride=count), :]
+        one = tiles_wide[pl.ds(t, HALF, stride=count + 1), :]
+        two = tiles_wide[pl.ds(t + 1, HALF, stride=count + 1), :]
         even = jnp.where(low_lanes, one, pltpu.roll(two, BS, 1))
         odd = jnp.where(low_lanes, pltpu.roll(one, BS, 1), two)
         turned = jnp.concatenate([even, odd], axis=0).astype(BF16).T
@@ -325,12 +325,6 @@
     if steps > 1:
         learn_finish(steps - 1)
     others(n_gy, gy, lambda j: totals_copy(j, gy).start())
-
-    others(n_gy, gy, lambda j: totals_copy(j, j).wait_recv())
-    total = jnp.zeros((NREG, LANES), F32)
-    for j in range(n_gy):
-        total = total + totals_in[j]
-    scale = 1.0 / jnp.maximum(total, 1.0)
 
     for k, (_, _, _, _, _, has_source) in enumerate(plans):
 
@@ -357,7 +351,7 @@
         strain = straight * (1.0 / math.sqrt(BS))
         rho = density_ref[t]
         sens = cross * (-(3.0 * rho * rho / (2.0 * math.sqrt(BS))))
-        at = pl.ds(pl.multiple_of(t * 8, 8), 8)
+        at = pl.ds(t * 9, 8)
         partial[at, :] = weight_ref[t] * jnp.where(low8, sens, strain)
         return strain
 
@@ -370,9 +364,9 @@
 
     comp = lax.fori_loop(0, count // unroll, elements, jnp.zeros((8, LANES), F32))
 
-    payload = partial[pl.ds(0, count, stride=8), :]
+    payload = partial[pl.ds(0, count, stride=9), :]
     for s in range(1, 8):
-        payload = payload + partial[pl.ds(s, count, stride=8), :]
+        payload = payload + partial[pl.ds(s, count, stride=9), :]
     sums_out[:, 0:NREG, :] = rows_by_region(hot, payload).reshape(n_gy, NREG, LANES)
     for j in range(n_gy):
         sums_out[j, NREG : NREG + 8, :] = comp
@@ -385,6 +379,11 @@
     comp_out[...] = gathered[NREG : NREG + 8, :]
     comp_in[gx] = comp_out[...]
     others(n_gx, gx, lambda i: comp_copy(i, gx).start())
+    others(n_gy, gy, lambda j: totals_copy(j, j).wait_recv())
+    total = jnp.zeros((NREG, LANES), F32)
+    for j in range(n_gy):
+        total = total + totals_in[j]
+    scale = 1.0 / jnp.maximum(total, 1.0)
     filtered_ref[...] = gathered[0:NREG, :] * scale
 
     for k, (_, _, _, has_target, _, _) in enumerate(plans):
@@ -401,7 +400,8 @@
         0, n_gx, lambda i, acc: acc + comp_in[i], jnp.zeros((8, LANES), F32)
     )
     line = jnp.sum(everything, axis=0, keepdims=True) / math.sqrt(count * n_gx * n_gy)
-    compliance_ref[...] = pltpu.roll(jnp.broadcast_to(line, (8, LANES)), R, 1)[0:1, :]
+    turned_line = pltpu.roll(jnp.broadcast_to(line, (8, LANES)), R, 1)
+    compliance_ref[...] = turned_line[0, 0:R]
     others(n_gx, gx, lambda i: comp_copy(i, gx).wait_send())
 
 
@@ -430,7 +430,7 @@
         functools.partial(kernel, n_gx, n_gy),
         out_shape=(
             jax.ShapeDtypeStruct((NREG, LANES), F32),
-            jax.ShapeDtypeStruct((1, LANES), F32),
+            jax.ShapeDtypeStruct((R,), F32),
         ),
         in_specs=[hbm] * 11,
         out_specs=(vmem, vmem),
@@ -441,9 +441,9 @@
             pltpu.VMEM((blocks, BS * R), BF16),
             pltpu.VMEM((blocks, BS * R), BF16),
             pltpu.VMEM((count, BS * BS), BF16),
-            pltpu.VMEM((HALF * blocks, LANES), F32),
-            pltpu.VMEM((HALF * blocks, LANES), F32),
-            pltpu.VMEM((HALF * count, LANES), F32),
+            pltpu.VMEM((HALF * (blocks + 1), LANES), F32),
+            pltpu.VMEM((HALF * (blocks + 1), LANES), F32),
+            pltpu.VMEM((HALF * (count + 1), LANES), F32),
             pltpu.VMEM((blocks, BS, 2 * LANES), BF16),
             pltpu.VMEM((blocks + faces, BS, LANES), BF16),
             pltpu.VMEM((faces, BS, LANES), BF16),
@@ -451,7 +451,7 @@
             pltpu.VMEM((count * BS, LANES), F32),
             pltpu.VMEM((count, n_gy * NREG), F32),
             pltpu.VMEM((count, LANES), F32),
-            pltpu.VMEM((count * 8, LANES), F32),
+            pltpu.VMEM((count * 9, LANES), F32),
             pltpu.VMEM((8, LANES), F32),
             pltpu.VMEM((n_gy, NREG, LANES), F32),
             pltpu.VMEM((n_gy, NREG, LANES), F32),
@@ -489,7 +489,7 @@
         adjoint,
         tiles,
     )
-    return filtered, compliance[0, :R]
+    return filtered, compliance
 
 
 def solution(mesh):

time: 35.7 us -> 29.5 us (0.83)
  Pallas kernels: 32.3 us -> 26.8 us
  local copies, waits for them, and re-layouts: 2.49 us -> 1.84 us
    pallas_call x1, Pallas kernels: 32.3 us -> 26.8 us  [shards(): pl.pallas_call(functools.partial(kernel, n_gx, n_gy), out_shape=(jax.Shap...]
    squeeze x1 -> x0, local copies, waits for them, and re-layouts: 0.51 us -> none  [shards(): return (filtered, compliance[0, :R])]
    unnamed x3 -> x4, local copies, waits for them, and re-layouts: 1.98 us -> 1.84 us
where the time goes in v3:
time: 29.5 us; the launch traced here: 29.3 us
  Pallas kernels  26.8 us (91%)
  local copies, waits for them, and re-layouts  1.84 us (6%)
  between operations  0.65 us (2%)
    pallas_call x1, Pallas kernels, shards(): pl.pallas_call(functools.partial(kernel, n_gx, n_gy), out_shape=(jax.Shap...  26.8 us
    unnamed x4, local copies, waits for them, and re-layouts  1.84 us

profile of v3, /device:TPU:0, one launch (start us, length us, event | category | flops | bytes accessed | tf_op | source)
XLA Modules:
  0.0 29.3 jit_solution(9171371266282480644)
XLA Ops:
  0.6 26.8 %sensitivities.1 = (f32[32,128]{1,0:T(8,128)}, f32[64]{0:T(128)}) custom-call(s32[96]{0:T(128)} %rows_hbm.1, s32[96]{0:T(128)} %cols_hbm.1, f32[96]{0:T(128)} %density_hbm.1, f32[96]{0:T(128)} %weight_hbm.1, s32[96]{0:T(128)} %bitcast.1, s32[96]{0:T(128)} %region_hbm.1, s32[1,2,12]{2,1,0:T(2,128)} %face_x_hbm.1, s32[1,2,4]{2,1,0:T(2,128)} %face_y_hbm.1, ...), custom_call_target="tpu_custom_call" | custom-call | tf_op jit(solution)/shard_map/sensitivities/pallas_call | solution.py:429
  27.4 0.0 copy-start
  27.4 1.3 %copy.15 = f32[32,128]{1,0:T(8,128)} copy(f32[32,128]{1,0:T(8,128)} %get-tuple-element.4) | data formatting | bytes 32768
  28.8 0.0 copy-done
  28.8 0.5 %copy.16 = f32[64]{0:T(128)} copy(f32[64]{0:T(128)S(1)} %copy-done) | data formatting | bytes 512
Async XLA Ops:
  27.4 1.3 %copy-start = (f32[64]{0:T(128)S(1)}, f32[64]{0:T(128)}, u32[]{:S(2)}) copy-start(f32[64]{0:T(128)} %get-tuple-element.5) | copy-start | bytes 772

commit v4 on v3

--- a/solution.py
+++ b/solution.py
@@ -19,10 +19,12 @@
 I32 = jnp.int32
 
 
-def loop(count, unroll, body):
+def loop(count, unroll, read, write):
     def step(i, carry):
-        for k in range(unroll):
-            body(i * unroll + k)
+        places = [i * unroll + k for k in range(unroll)]
+        values = [read(place) for place in places]
+        for place, value in zip(places, values):
+            write(place, value)
         return carry
 
     lax.fori_loop(0, count // unroll, step, 0)
@@ -82,6 +84,7 @@
     disp_wide,
     adj_wide,
     tiles_wide,
+    turned,
     local,
     ext,
     staged,
@@ -181,11 +184,14 @@
     steps = (max(n_gx, n_gy) - 1).bit_length()
 
     def widen(raw, wide, height):
-        def body(c):
-            chunk = raw[:, pl.ds(pl.multiple_of(c * LANES, LANES), LANES)]
-            wide[pl.ds(c * (height + 1), height), :] = chunk.astype(F32)
-
-        loop(HALF, 4, body)
+        def read(c):
+            at = pl.ds(pl.multiple_of(c * LANES, LANES), LANES)
+            return raw[:, at].astype(F32)
+
+        def write(c, chunk):
+            wide[pl.ds(c * (height + 1), height), :] = chunk
+
+        loop(HALF, 4, read, write)
 
     low_lanes = lax.broadcasted_iota(jnp.int32, (HALF, LANES), 1) < R
 
@@ -207,17 +213,17 @@
         swapped = jnp.concatenate([even_swapped, odd_swapped], axis=0).astype(BF16)
         return block, swapped
 
-    def local_block(b):
-        block, swapped = parts(b)
+    def keep_local(b, pair):
+        block, swapped = pair
         local[b, :, 0:LANES] = block
         local[b, :, LANES : 2 * LANES] = swapped
         ext[b] = block
 
     def stage(faces, way, at, number):
-        def body(k):
-            staged[at + k] = parts(faces[0, way, k])[0]
-
-        loop(number, 4, body)
+        def write(k, block):
+            staged[at + k] = block
+
+        loop(number, 4, lambda k: parts(faces[0, way, k])[0], write)
 
     first = blocks
     plans = (
@@ -259,7 +265,7 @@
             ext[pl.ds(to, number)] = jnp.zeros((number, BS, LANES), BF16)
 
     learn_start(0)
-    loop(blocks, 4, local_block)
+    loop(blocks, 4, parts, keep_local)
     learn_finish(0)
     for step in range(1, steps):
         learn_start(step)
@@ -273,10 +279,13 @@
 
     def key_row(t):
         key = owner_ref[t] * NREG + region_ref[t]
-        onehot[pl.ds(t, 1), :] = (key_lane == key).astype(F32)
-        weights[pl.ds(t, 1), :] = jnp.full((1, LANES), weight_ref[t], F32)
-
-    loop(count, 4, key_row)
+        return (key_lane == key).astype(F32), jnp.full((1, LANES), weight_ref[t], F32)
+
+    def keep_key(t, rows):
+        onehot[pl.ds(t, 1), :] = rows[0]
+        weights[pl.ds(t, 1), :] = rows[1]
+
+    loop(count, 8, key_row, keep_key)
     hot = onehot[...].astype(BF16)
     totals_out[...] = rows_by_region(hot, weights[...]).reshape(n_gy, NREG, LANES)
     totals_in[gy] = totals_out[gy]
@@ -304,24 +313,37 @@
     loads[2].wait()
     widen(tiles_raw, tiles_wide, count)
 
-    def products(i):
+    def turn(i):
         t = 2 * i
         one = tiles_wide[pl.ds(t, HALF, stride=count + 1), :]
         two = tiles_wide[pl.ds(t + 1, HALF, stride=count + 1), :]
         even = jnp.where(low_lanes, one, pltpu.roll(two, BS, 1))
         odd = jnp.where(low_lanes, pltpu.roll(one, BS, 1), two)
-        turned = jnp.concatenate([even, odd], axis=0).astype(BF16).T
-        for k in range(2):
-            result = jnp.dot(
-                turned[k * BS : (k + 1) * BS, :],
-                local[rows_ref[t + k]],
-                preferred_element_type=F32,
-            )
-            at = pl.ds(pl.multiple_of((t + k) * BS, BS), BS)
-            prod[at, :] = result[:, 0:LANES]
-            prod_swapped[at, :] = result[:, LANES : 2 * LANES]
-
-    loop(count // 2, 2, products)
+        return jnp.concatenate([even, odd], axis=0).astype(BF16).T
+
+    def keep_turned(i, value):
+        turned[i] = value
+
+    loop(count // 2, 4, turn, keep_turned)
+
+    def product(t, i, k):
+        return jnp.dot(
+            turned[i, k * BS : (k + 1) * BS, :], local[rows_ref[t]], preferred_element_type=F32
+        )
+
+    def keep_product(t, result):
+        at = pl.ds(pl.multiple_of(t * BS, BS), BS)
+        prod[at, :] = result[:, 0:LANES]
+        prod_swapped[at, :] = result[:, LANES : 2 * LANES]
+
+    def product_pair(i):
+        return product(2 * i, i, 0), product(2 * i + 1, i, 1)
+
+    def keep_pair(i, results):
+        keep_product(2 * i, results[0])
+        keep_product(2 * i + 1, results[1])
+
+    loop(count // 2, 2, product_pair, keep_pair)
     if steps > 1:
         learn_finish(steps - 1)
     others(n_gy, gy, lambda j: totals_copy(j, gy).start())
@@ -350,16 +372,16 @@
         cross = crossed + pltpu.roll(crossed, R, 1)
         strain = straight * (1.0 / math.sqrt(BS))
         rho = density_ref[t]
-        sens = cross * (-(3.0 * rho * rho / (2.0 * math.sqrt(BS))))
-        at = pl.ds(t * 9, 8)
-        partial[at, :] = weight_ref[t] * jnp.where(low8, sens, strain)
-        return strain
-
-    unroll = 4
+        sens = cross * (rho * rho * (-3.0 / (2.0 * math.sqrt(BS))))
+        return weight_ref[t] * jnp.where(low8, sens, strain), strain
+
+    unroll = 8
 
     def elements(i, total_energy):
-        for k in range(unroll):
-            total_energy = total_energy + element(i * unroll + k)
+        values = [element(i * unroll + k) for k in range(unroll)]
+        for k, (value, strain) in enumerate(values):
+            partial[pl.ds((i * unroll + k) * 9, 8), :] = value
+            total_energy = total_energy + strain
         return total_energy
 
     comp = lax.fori_loop(0, count // unroll, elements, jnp.zeros((8, LANES), F32))
@@ -444,6 +466,7 @@
             pltpu.VMEM((HALF * (blocks + 1), LANES), F32),
             pltpu.VMEM((HALF * (blocks + 1), LANES), F32),
             pltpu.VMEM((HALF * (count + 1), LANES), F32),
+            pltpu.VMEM((count // 2, 2 * BS, BS), BF16),
             pltpu.VMEM((blocks, BS, 2 * LANES), BF16),
             pltpu.VMEM((blocks + faces, BS, LANES), BF16),
             pltpu.VMEM((faces, BS, LANES), BF16),
@@ -473,10 +496,10 @@
             pltpu.SemaphoreType.REGULAR((steps, 2)),
         ],
         compiler_params=pltpu.CompilerParams(
-            collective_id=0, has_side_effects=True, vmem_limit_bytes=60 * 2**20
+            collective_id=0, has_side_effects=True, vmem_limit_bytes=40 * 2**20
         ),
         name="sensitivities",
-    )(
+    )(*[pltpu.with_memory_space_constraint(x, pltpu.HBM) for x in (
         tile_rows,
         tile_cols,
         density,
@@ -488,7 +511,7 @@
         disp,
         adjoint,
         tiles,
-    )
+    )])
     return filtered, compliance
 
 

time: 29.5 us -> 26.2 us (0.89)
  Pallas kernels: 26.8 us -> 24.3 us
  local copies, waits for them, and re-layouts: 1.84 us -> 1.12 us
    pallas_call x1, Pallas kernels: 26.8 us -> 24.3 us  [shards(): pl.pallas_call(functools.partial(kernel, n_gx, n_gy), out_shape=(jax.Shap...]
    unnamed x4 -> x2, local copies, waits for them, and re-layouts: 1.84 us -> 1.12 us
where the time goes in v4:
time: 26.2 us; the launch traced here: 26.1 us
  Pallas kernels  24.3 us (93%)
  local copies, waits for them, and re-layouts  1.12 us (4%)
  between operations  0.64 us (2%)
    pallas_call x1, Pallas kernels, shards(): pl.pallas_call(functools.partial(kernel, n_gx, n_gy), out_shape=(jax.Shap...  24.3 us
    unnamed x2, local copies, waits for them, and re-layouts  1.12 us

profile of v4, /device:TPU:0, one launch (start us, length us, event | category | flops | bytes accessed | tf_op | source)
XLA Modules:
  0.0 26.1 jit_solution(8454995083300132642)
XLA Ops:
  0.6 24.3 %sensitivities.1 = (f32[32,128]{1,0:T(8,128)S(1)}, f32[64]{0:T(128)S(1)}) custom-call(s32[96]{0:T(128)} %rows_hbm.1, s32[96]{0:T(128)} %cols_hbm.1, f32[96]{0:T(128)} %density_hbm.1, f32[96]{0:T(128)} %weight_hbm.1, s32[96]{0:T(128)} %bitcast.1, s32[96]{0:T(128)} %region_hbm.1, s32[1,2,12]{2,1,0:T(2,128)} %face_x_hbm.1, s32[1,2,4]{2,1,0:T(2,128)} %face_y_hbm.1, ...), custom_call_target="tpu_custom_call" | custom-call | tf_op jit(solution)/shard_map/sensitivities/pallas_call | solution.py:451
  25.0 0.6 %copy.15 = f32[32,128]{1,0:T(8,128)} copy(f32[32,128]{1,0:T(8,128)S(1)} %get-tuple-element.4) | data formatting | bytes 32768
  25.6 0.5 %copy.16 = f32[64]{0:T(128)} copy(f32[64]{0:T(128)S(1)} %get-tuple-element.5) | data formatting | bytes 512

commit v5 on v4

--- a/solution.py
+++ b/solution.py
@@ -47,11 +47,16 @@
     return jnp.concatenate([high, low], axis=0)
 
 
-def rows_by_region(onehot, x):
-    doubled = jnp.concatenate([onehot, onehot], axis=0)
-    return lax.dot_general(
-        doubled, two_terms(x), (((0,), (0,)), ((), ())), preferred_element_type=F32
-    )
+def rows_by_region(hot_turned, x):
+    return jnp.dot(hot_turned, two_terms(x), preferred_element_type=F32)
+
+
+def knowledge_rounds(n_gx, n_gy):
+    return [
+        (along, 2**step)
+        for along, size in ((1, n_gy), (0, n_gx))
+        for step in range((size - 1).bit_length())
+    ]
 
 
 def kernel(
@@ -91,9 +96,9 @@
     prod,
     prod_swapped,
     onehot,
+    hot_turned,
     weights,
     partial,
-    energy,
     totals_out,
     totals_in,
     sums_out,
@@ -110,9 +115,9 @@
     comp_send,
     comp_recv,
     scalar_sem,
-    known_x,
-    known_y,
+    known,
 ):
+    rounds = knowledge_rounds(n_gx, n_gy)
     count = tiles_hbm.shape[0]
     blocks = disp_hbm.shape[0]
     nix = face_x_ref.shape[2]
@@ -165,23 +170,26 @@
     for load in loads[:2] + scalar_loads + loads[2:]:
         load.start()
 
-    def learn_start(step):
+    def learn(step, act):
+        along, distance = rounds[step]
+
         def body(side, way, where):
-            known = known_x if side == 0 else known_y
-            pl.semaphore_signal(
-                known.at[step, way], inc=1, device_id=where, device_id_type=MESH
-            )
-
-        each_way(2**step, body)
-
-    def learn_finish(step):
-        def body(side, way, where):
-            known = known_x if side == 0 else known_y
-            pl.semaphore_wait(known.at[step, 1 - way], 1)
-
-        each_way(2**step, body)
-
-    steps = (max(n_gx, n_gy) - 1).bit_length()
+            if side == along:
+                act(step, way, where)
+
+        each_way(distance, body)
+
+    def tell(step, way, where):
+        pl.semaphore_signal(known.at[step, way], inc=1, device_id=where, device_id_type=MESH)
+
+    def hear(step, way, where):
+        pl.semaphore_wait(known.at[step, 1 - way], 1)
+
+    def next_round(step):
+        if step > 0:
+            learn(step - 1, hear)
+        if step < len(rounds):
+            learn(step, tell)
 
     def widen(raw, wide, height):
         def read(c):
@@ -245,9 +253,10 @@
 
     for load in scalar_loads[:2]:
         load.wait()
-    for k, (at, to, number, has_target, _, has_source) in enumerate(plans):
+    for k in (1, 0, 2, 3):
+        at, to, number, has_target, _, has_source = plans[k]
         stage(face_x_ref if k < 2 else face_y_ref, k % 2, at, number)
-        if k == 0:
+        if k == 1:
             neighbours = (
                 (gx > 0).astype(jnp.int32)
                 + (gx < n_gx - 1).astype(jnp.int32)
@@ -264,13 +273,11 @@
         def _(to=to, number=number):
             ext[pl.ds(to, number)] = jnp.zeros((number, BS, LANES), BF16)
 
-    learn_start(0)
+        if k == 1:
+            next_round(0)
+
     loop(blocks, 4, parts, keep_local)
-    learn_finish(0)
-    for step in range(1, steps):
-        learn_start(step)
-        if step < steps - 1:
-            learn_finish(step)
+    next_round(1)
     for load in scalar_loads[2:]:
         load.wait()
 
@@ -287,8 +294,10 @@
 
     loop(count, 8, key_row, keep_key)
     hot = onehot[...].astype(BF16)
-    totals_out[...] = rows_by_region(hot, weights[...]).reshape(n_gy, NREG, LANES)
+    hot_turned[...] = jnp.concatenate([hot, hot], axis=0).T
+    totals_out[...] = rows_by_region(hot_turned[...], weights[...]).reshape(n_gy, NREG, LANES)
     totals_in[gy] = totals_out[gy]
+    next_round(2)
 
     def totals_copy(j, slot):
         return exchange(
@@ -300,15 +309,21 @@
             sums_out.at[j], sums_in.at[slot], sums_send.at[j], sums_recv.at[slot], (gx, j)
         )
 
-    def comp_copy(i, slot):
-        return exchange(comp_out, comp_in.at[slot], comp_send.at[i], comp_recv.at[slot], (i, gy))
-
-    def others(size, me, body):
-        @pl.loop(0, size)
-        def _(i):
-            @pl.when(i != me)
-            def _():
-                body(i)
+    me = gx * n_gy + gy
+
+    def comp_copy(d, slot):
+        return exchange(
+            comp_out,
+            comp_in.at[slot],
+            comp_send.at[d],
+            comp_recv.at[slot],
+            (lax.div(d, n_gy), lax.rem(d, n_gy)),
+        )
+
+    def others(size, own, body):
+        @pl.loop(1, size)
+        def _(offset):
+            body(lax.rem(own + offset, size))
 
     loads[2].wait()
     widen(tiles_raw, tiles_wide, count)
@@ -325,6 +340,7 @@
         turned[i] = value
 
     loop(count // 2, 4, turn, keep_turned)
+    next_round(3)
 
     def product(t, i, k):
         return jnp.dot(
@@ -343,9 +359,9 @@
         keep_product(2 * i, results[0])
         keep_product(2 * i + 1, results[1])
 
-    loop(count // 2, 2, product_pair, keep_pair)
-    if steps > 1:
-        learn_finish(steps - 1)
+    loop(count // 2, 4, product_pair, keep_pair)
+    for step in range(4, len(rounds)):
+        next_round(step)
     others(n_gy, gy, lambda j: totals_copy(j, gy).start())
 
     for k, (_, _, _, _, _, has_source) in enumerate(plans):
@@ -386,45 +402,51 @@
 
     comp = lax.fori_loop(0, count // unroll, elements, jnp.zeros((8, LANES), F32))
 
+    next_round(len(rounds))
+    comp_out[...] = jnp.sum(comp, axis=0, keepdims=True)
+    comp_in[me] = comp_out[...]
+    others(n_gx * n_gy, me, lambda d: comp_copy(d, me).start())
+
     payload = partial[pl.ds(0, count, stride=9), :]
     for s in range(1, 8):
         payload = payload + partial[pl.ds(s, count, stride=9), :]
-    sums_out[:, 0:NREG, :] = rows_by_region(hot, payload).reshape(n_gy, NREG, LANES)
-    for j in range(n_gy):
-        sums_out[j, NREG : NREG + 8, :] = comp
+    sums_out[...] = rows_by_region(hot_turned[...], payload).reshape(n_gy, NREG, LANES)
     sums_in[gy] = sums_out[gy]
     others(n_gy, gy, lambda j: sums_copy(j, gy).start())
-    others(n_gy, gy, lambda j: sums_copy(j, j).wait_recv())
-    gathered = sums_in[0]
-    for j in range(1, n_gy):
-        gathered = gathered + sums_in[j]
-    comp_out[...] = gathered[NREG : NREG + 8, :]
-    comp_in[gx] = comp_out[...]
-    others(n_gx, gx, lambda i: comp_copy(i, gx).start())
+
+    for k, (_, _, _, has_target, _, _) in enumerate(plans):
+
+        @pl.when(has_target)
+        def _(k=k):
+            halo(k).wait_send()
+
+    others(n_gy, gy, lambda j: totals_copy(j, gy).wait_send())
     others(n_gy, gy, lambda j: totals_copy(j, j).wait_recv())
     total = jnp.zeros((NREG, LANES), F32)
     for j in range(n_gy):
         total = total + totals_in[j]
     scale = 1.0 / jnp.maximum(total, 1.0)
-    filtered_ref[...] = gathered[0:NREG, :] * scale
-
-    for k, (_, _, _, has_target, _, _) in enumerate(plans):
-
-        @pl.when(has_target)
-        def _(k=k):
-            halo(k).wait_send()
-
-    others(n_gy, gy, lambda j: totals_copy(j, gy).wait_send())
+    others(n_gx * n_gy, me, lambda d: comp_copy(d, me).wait_send())
+
     others(n_gy, gy, lambda j: sums_copy(j, gy).wait_send())
-
-    others(n_gx, gx, lambda i: comp_copy(i, i).wait_recv())
-    everything = lax.fori_loop(
-        0, n_gx, lambda i, acc: acc + comp_in[i], jnp.zeros((8, LANES), F32)
-    )
-    line = jnp.sum(everything, axis=0, keepdims=True) / math.sqrt(count * n_gx * n_gy)
+    others(n_gy, gy, lambda j: sums_copy(j, j).wait_recv())
+    gathered = sums_in[0]
+    for j in range(1, n_gy):
+        gathered = gathered + sums_in[j]
+    filtered_ref[...] = gathered * scale
+
+    others(n_gx * n_gy, me, lambda d: comp_copy(d, d).wait_recv())
+    unroll = n_gy
+
+    def gather(i, acc):
+        for k in range(unroll):
+            acc = acc + comp_in[i * unroll + k]
+        return acc
+
+    line = lax.fori_loop(0, n_gx, gather, jnp.zeros((1, LANES), F32))
+    line = line * (1.0 / math.sqrt(count * n_gx * n_gy))
     turned_line = pltpu.roll(jnp.broadcast_to(line, (8, LANES)), R, 1)
     compliance_ref[...] = turned_line[0, 0:R]
-    others(n_gx, gx, lambda i: comp_copy(i, gx).wait_send())
 
 
 def shards(n_gx, n_gy, *args):
@@ -445,7 +467,6 @@
     blocks = disp.shape[0]
     faces = face_x.shape[2] * 2 + face_y.shape[2] * 2
     hbm = pl.BlockSpec(memory_space=pltpu.HBM)
-    steps = (max(n_gx, n_gy) - 1).bit_length()
     vmem = pl.BlockSpec(memory_space=pltpu.VMEM)
     dma = pltpu.SemaphoreType.DMA
     filtered, compliance = pl.pallas_call(
@@ -473,15 +494,12 @@
             pltpu.VMEM((count * BS, LANES), F32),
             pltpu.VMEM((count * BS, LANES), F32),
             pltpu.VMEM((count, n_gy * NREG), F32),
+            pltpu.VMEM((n_gy * NREG, 2 * count), BF16),
             pltpu.VMEM((count, LANES), F32),
             pltpu.VMEM((count * 9, LANES), F32),
-            pltpu.VMEM((8, LANES), F32),
-            pltpu.VMEM((n_gy, NREG, LANES), F32),
-            pltpu.VMEM((n_gy, NREG, LANES), F32),
-            pltpu.VMEM((n_gy, NREG + 8, LANES), F32),
-            pltpu.VMEM((n_gy, NREG + 8, LANES), F32),
-            pltpu.VMEM((8, LANES), F32),
-            pltpu.VMEM((n_gx, 8, LANES), F32),
+            *[pltpu.VMEM((n_gy, NREG, LANES), F32)] * 4,
+            pltpu.VMEM((1, LANES), F32),
+            pltpu.VMEM((n_gx * n_gy, 1, LANES), F32),
             dma((3,)),
             dma((4,)),
             dma((4,)),
@@ -489,11 +507,10 @@
             dma((n_gy,)),
             dma((n_gy,)),
             dma((n_gy,)),
-            dma((n_gx,)),
-            dma((n_gx,)),
+            dma((n_gx * n_gy,)),
+            dma((n_gx * n_gy,)),
             dma((8,)),
-            pltpu.SemaphoreType.REGULAR((steps, 2)),
-            pltpu.SemaphoreType.REGULAR((steps, 2)),
+            pltpu.SemaphoreType.REGULAR((len(knowledge_rounds(n_gx, n_gy)), 2)),
         ],
         compiler_params=pltpu.CompilerParams(
             collective_id=0, has_side_effects=True, vmem_limit_bytes=40 * 2**20

time: 26.2 us -> 24.1 us (0.920)
  Pallas kernels: 24.3 us -> 22.2 us
    pallas_call x1, Pallas kernels: 24.3 us -> 22.2 us  [shards(): pl.pallas_call(functools.partial(kernel, n_gx, n_gy), out_shape=(jax.Shap...]
where the time goes in v5:
time: 24.1 us; the launch traced here: 24 us
  Pallas kernels  22.2 us (92%)
  local copies, waits for them, and re-layouts  1.12 us (5%)
  between operations  0.64 us (3%)
    pallas_call x1, Pallas kernels, shards(): pl.pallas_call(functools.partial(kernel, n_gx, n_gy), out_shape=(jax.Shap...  22.2 us
    unnamed x2, local copies, waits for them, and re-layouts  1.12 us

profile of v5, /device:TPU:0, one launch (start us, length us, event | category | flops | bytes accessed | tf_op | source)
XLA Modules:
  0.0 24.0 jit_solution(7654697772932680186)
XLA Ops:
  0.6 22.2 %sensitivities.1 = (f32[32,128]{1,0:T(8,128)S(1)}, f32[64]{0:T(128)S(1)}) custom-call(s32[96]{0:T(128)} %rows_hbm.1, s32[96]{0:T(128)} %cols_hbm.1, f32[96]{0:T(128)} %density_hbm.1, f32[96]{0:T(128)} %weight_hbm.1, s32[96]{0:T(128)} %bitcast.1, s32[96]{0:T(128)} %region_hbm.1, s32[1,2,12]{2,1,0:T(2,128)} %face_x_hbm.1, s32[1,2,4]{2,1,0:T(2,128)} %face_y_hbm.1, ...), custom_call_target="tpu_custom_call" | custom-call | tf_op jit(solution)/shard_map/sensitivities/pallas_call | solution.py:472
  22.9 0.6 %copy.15 = f32[32,128]{1,0:T(8,128)} copy(f32[32,128]{1,0:T(8,128)S(1)} %get-tuple-element.4) | data formatting | bytes 32768
  23.5 0.5 %copy.16 = f32[64]{0:T(128)} copy(f32[64]{0:T(128)S(1)} %get-tuple-element.5) | data formatting | bytes 512

commit v6 on v5

--- a/solution.py
+++ b/solution.py
@@ -167,7 +167,7 @@
             )
         )
     ]
-    for load in loads[:2] + scalar_loads + loads[2:]:
+    for load in scalar_loads[5:] + loads[:2] + scalar_loads[:5] + loads[2:]:
         load.start()
 
     def learn(step, act):
@@ -202,6 +202,21 @@
         loop(HALF, 4, read, write)
 
     low_lanes = lax.broadcasted_iota(jnp.int32, (HALF, LANES), 1) < R
+
+    for load in scalar_loads[5:]:
+        load.wait()
+    regions = n_gy * NREG
+    key_lane = lax.broadcasted_iota(jnp.int32, (1, regions), 1)
+
+    def key_row(t):
+        key = owner_ref[t] * NREG + region_ref[t]
+        return (key_lane == key).astype(F32), jnp.full((1, LANES), weight_ref[t], F32)
+
+    def keep_key(t, rows):
+        onehot[pl.ds(t, 1), :] = rows[0]
+        weights[pl.ds(t, 1), :] = rows[1]
+
+    loop(count, 8, key_row, keep_key)
 
     loads[0].wait()
     widen(disp_raw, disp_wide, blocks)
@@ -253,17 +268,22 @@
 
     for load in scalar_loads[:2]:
         load.wait()
-    for k in (1, 0, 2, 3):
-        at, to, number, has_target, _, has_source = plans[k]
-        stage(face_x_ref if k < 2 else face_y_ref, k % 2, at, number)
-        if k == 1:
-            neighbours = (
-                (gx > 0).astype(jnp.int32)
-                + (gx < n_gx - 1).astype(jnp.int32)
-                + (gy > 0).astype(jnp.int32)
-                + (gy < n_gy - 1).astype(jnp.int32)
-            )
-            pl.semaphore_wait(barrier, neighbours)
+    for k in (1, 0, 3, 2):
+        at, _, number, has_target, _, _ = plans[k]
+
+        @pl.when(has_target)
+        def _(k=k, at=at, number=number):
+            stage(face_x_ref if k < 2 else face_y_ref, k % 2, at, number)
+
+    neighbours = (
+        (gx > 0).astype(jnp.int32)
+        + (gx < n_gx - 1).astype(jnp.int32)
+        + (gy > 0).astype(jnp.int32)
+        + (gy < n_gy - 1).astype(jnp.int32)
+    )
+    pl.semaphore_wait(barrier, neighbours)
+    for k in (1, 0, 3, 2):
+        _, to, number, has_target, _, has_source = plans[k]
 
         @pl.when(has_target)
         def _(k=k):
@@ -273,26 +293,12 @@
         def _(to=to, number=number):
             ext[pl.ds(to, number)] = jnp.zeros((number, BS, LANES), BF16)
 
-        if k == 1:
-            next_round(0)
-
+    next_round(0)
     loop(blocks, 4, parts, keep_local)
     next_round(1)
-    for load in scalar_loads[2:]:
+    for load in scalar_loads[2:5]:
         load.wait()
 
-    regions = n_gy * NREG
-    key_lane = lax.broadcasted_iota(jnp.int32, (1, regions), 1)
-
-    def key_row(t):
-        key = owner_ref[t] * NREG + region_ref[t]
-        return (key_lane == key).astype(F32), jnp.full((1, LANES), weight_ref[t], F32)
-
-    def keep_key(t, rows):
-        onehot[pl.ds(t, 1), :] = rows[0]
-        weights[pl.ds(t, 1), :] = rows[1]
-
-    loop(count, 8, key_row, keep_key)
     hot = onehot[...].astype(BF16)
     hot_turned[...] = jnp.concatenate([hot, hot], axis=0).T
     totals_out[...] = rows_by_region(hot_turned[...], weights[...]).reshape(n_gy, NREG, LANES)
@@ -315,10 +321,14 @@
         return exchange(
             comp_out,
             comp_in.at[slot],
-            comp_send.at[d],
-            comp_recv.at[slot],
+            comp_send,
+            comp_recv,
             (lax.div(d, n_gy), lax.rem(d, n_gy)),
         )
+
+    def all_rows(sem):
+        rows = comp_in.at[pl.ds(0, n_gx * n_gy - 1)]
+        return pltpu.make_async_copy(rows, rows, sem)
 
     def others(size, own, body):
         @pl.loop(1, size)
@@ -426,7 +436,7 @@
     for j in range(n_gy):
         total = total + totals_in[j]
     scale = 1.0 / jnp.maximum(total, 1.0)
-    others(n_gx * n_gy, me, lambda d: comp_copy(d, me).wait_send())
+    all_rows(comp_send).wait()
 
     others(n_gy, gy, lambda j: sums_copy(j, gy).wait_send())
     others(n_gy, gy, lambda j: sums_copy(j, j).wait_recv())
@@ -435,7 +445,7 @@
         gathered = gathered + sums_in[j]
     filtered_ref[...] = gathered * scale
 
-    others(n_gx * n_gy, me, lambda d: comp_copy(d, d).wait_recv())
+    all_rows(comp_recv).wait()
     unroll = n_gy
 
     def gather(i, acc):
@@ -507,8 +517,8 @@
             dma((n_gy,)),
             dma((n_gy,)),
             dma((n_gy,)),
-            dma((n_gx * n_gy,)),
-            dma((n_gx * n_gy,)),
+            dma,
+            dma,
             dma((8,)),
             pltpu.SemaphoreType.REGULAR((len(knowledge_rounds(n_gx, n_gy)), 2)),
         ],

time: 24.1 us -> 23.7 us (0.983)
  Pallas kernels: 22.2 us -> 21.8 us
    pallas_call x1, Pallas kernels: 22.2 us -> 21.8 us  [shards(): pl.pallas_call(functools.partial(kernel, n_gx, n_gy), out_shape=(jax.Shap...]
where the time goes in v6:
time: 23.7 us; the launch traced here: 23.5 us
  Pallas kernels  21.8 us (92%)
  local copies, waits for them, and re-layouts  1.12 us (5%)
  between operations  0.64 us (3%)
    pallas_call x1, Pallas kernels, shards(): pl.pallas_call(functools.partial(kernel, n_gx, n_gy), out_shape=(jax.Shap...  21.8 us
    unnamed x2, local copies, waits for them, and re-layouts  1.12 us

profile of v6, /device:TPU:0, one launch (start us, length us, event | category | flops | bytes accessed | tf_op | source)
XLA Modules:
  0.0 23.5 jit_solution(15228198585744716870)
XLA Ops:
  0.6 21.8 %sensitivities.1 = (f32[32,128]{1,0:T(8,128)S(1)}, f32[64]{0:T(128)S(1)}) custom-call(s32[96]{0:T(128)} %rows_hbm.1, s32[96]{0:T(128)} %cols_hbm.1, f32[96]{0:T(128)} %density_hbm.1, f32[96]{0:T(128)} %weight_hbm.1, s32[96]{0:T(128)} %bitcast.1, s32[96]{0:T(128)} %region_hbm.1, s32[1,2,12]{2,1,0:T(2,128)} %face_x_hbm.1, s32[1,2,4]{2,1,0:T(2,128)} %face_y_hbm.1, ...), custom_call_target="tpu_custom_call" | custom-call | tf_op jit(solution)/shard_map/sensitivities/pallas_call | solution.py:482
  22.4 0.6 %copy.15 = f32[32,128]{1,0:T(8,128)} copy(f32[32,128]{1,0:T(8,128)S(1)} %get-tuple-element.4) | data formatting | bytes 32768
  23.0 0.5 %copy.16 = f32[64]{0:T(128)} copy(f32[64]{0:T(128)S(1)} %get-tuple-element.5) | data formatting | bytes 512

commit v7 on v5

--- a/solution.py
+++ b/solution.py
@@ -253,16 +253,20 @@
 
     for load in scalar_loads[:2]:
         load.wait()
-    for k in (1, 0, 2, 3):
+    neighbours = (
+        (gx > 0).astype(jnp.int32)
+        + (gx < n_gx - 1).astype(jnp.int32)
+        + (gy > 0).astype(jnp.int32)
+        + (gy < n_gy - 1).astype(jnp.int32)
+    )
+    for k in (1, 0, 3, 2):
         at, to, number, has_target, _, has_source = plans[k]
-        stage(face_x_ref if k < 2 else face_y_ref, k % 2, at, number)
+
+        @pl.when(has_target)
+        def _(k=k, at=at, number=number):
+            stage(face_x_ref if k < 2 else face_y_ref, k % 2, at, number)
+
         if k == 1:
-            neighbours = (
-                (gx > 0).astype(jnp.int32)
-                + (gx < n_gx - 1).astype(jnp.int32)
-                + (gy > 0).astype(jnp.int32)
-                + (gy < n_gy - 1).astype(jnp.int32)
-            )
             pl.semaphore_wait(barrier, neighbours)
 
         @pl.when(has_target)
@@ -273,9 +277,7 @@
         def _(to=to, number=number):
             ext[pl.ds(to, number)] = jnp.zeros((number, BS, LANES), BF16)
 
-        if k == 1:
-            next_round(0)
-
+    next_round(0)
     loop(blocks, 4, parts, keep_local)
     next_round(1)
     for load in scalar_loads[2:]:
@@ -315,10 +317,14 @@
         return exchange(
             comp_out,
             comp_in.at[slot],
-            comp_send.at[d],
-            comp_recv.at[slot],
+            comp_send,
+            comp_recv,
             (lax.div(d, n_gy), lax.rem(d, n_gy)),
         )
+
+    def all_rows(sem):
+        rows = comp_in.at[pl.ds(0, n_gx * n_gy - 1)]
+        return pltpu.make_async_copy(rows, rows, sem)
 
     def others(size, own, body):
         @pl.loop(1, size)
@@ -426,7 +432,7 @@
     for j in range(n_gy):
         total = total + totals_in[j]
     scale = 1.0 / jnp.maximum(total, 1.0)
-    others(n_gx * n_gy, me, lambda d: comp_copy(d, me).wait_send())
+    all_rows(comp_send).wait()
 
     others(n_gy, gy, lambda j: sums_copy(j, gy).wait_send())
     others(n_gy, gy, lambda j: sums_copy(j, j).wait_recv())
@@ -435,7 +441,7 @@
         gathered = gathered + sums_in[j]
     filtered_ref[...] = gathered * scale
 
-    others(n_gx * n_gy, me, lambda d: comp_copy(d, d).wait_recv())
+    all_rows(comp_recv).wait()
     unroll = n_gy
 
     def gather(i, acc):
@@ -507,8 +513,8 @@
             dma((n_gy,)),
             dma((n_gy,)),
             dma((n_gy,)),
-            dma((n_gx * n_gy,)),
-            dma((n_gx * n_gy,)),
+            dma,
+            dma,
             dma((8,)),
             pltpu.SemaphoreType.REGULAR((len(knowledge_rounds(n_gx, n_gy)), 2)),
         ],

time: 24.1 us -> 23.6 us (0.979)
  Pallas kernels: 22.2 us -> 21.7 us
    pallas_call x1, Pallas kernels: 22.2 us -> 21.7 us  [shards(): pl.pallas_call(functools.partial(kernel, n_gx, n_gy), out_shape=(jax.Shap...]
where the time goes in v7:
time: 23.6 us; the launch traced here: 23.4 us
  Pallas kernels  21.7 us (92%)
  local copies, waits for them, and re-layouts  1.12 us (5%)
  between operations  0.64 us (3%)
    pallas_call x1, Pallas kernels, shards(): pl.pallas_call(functools.partial(kernel, n_gx, n_gy), out_shape=(jax.Shap...  21.7 us
    unnamed x2, local copies, waits for them, and re-layouts  1.12 us

profile of v7, /device:TPU:0, one launch (start us, length us, event | category | flops | bytes accessed | tf_op | source)
XLA Modules:
  0.0 23.4 jit_solution(16484649197185042148)
XLA Ops:
  0.6 21.7 %sensitivities.1 = (f32[32,128]{1,0:T(8,128)S(1)}, f32[64]{0:T(128)S(1)}) custom-call(s32[96]{0:T(128)} %rows_hbm.1, s32[96]{0:T(128)} %cols_hbm.1, f32[96]{0:T(128)} %density_hbm.1, f32[96]{0:T(128)} %weight_hbm.1, s32[96]{0:T(128)} %bitcast.1, s32[96]{0:T(128)} %region_hbm.1, s32[1,2,12]{2,1,0:T(2,128)} %face_x_hbm.1, s32[1,2,4]{2,1,0:T(2,128)} %face_y_hbm.1, ...), custom_call_target="tpu_custom_call" | custom-call | tf_op jit(solution)/shard_map/sensitivities/pallas_call | solution.py:478
  22.3 0.6 %copy.15 = f32[32,128]{1,0:T(8,128)} copy(f32[32,128]{1,0:T(8,128)S(1)} %get-tuple-element.4) | data formatting | bytes 32768
  22.9 0.5 %copy.16 = f32[64]{0:T(128)} copy(f32[64]{0:T(128)S(1)} %get-tuple-element.5) | data formatting | bytes 512
